TPU v7x, 256 devices: a whole 4x4x8 slice. The times are simulated.
256 devices in a mesh: ctx: 64 (over z, y, core), kv: 4 (over x).
Axes of the slice: x: 4, y: 4, z: 8, core: 2. Of those that a mesh axis runs over, the one named last changes fastest.
Arguments:
- queries: bfloat16 [4, 64, 128], P(None, 'kv'), may hold values from -72 to 72
- keys: bfloat16 [2048, 4, 512, 128], P('ctx', 'kv'), may hold values from -15 to 15
- values: bfloat16 [2048, 4, 512, 128], P('ctx', 'kv'), may hold values from -24 to 24
- lengths: int32 [4], replicated, may hold values from 512 to 262144, as said below
- span_map: int32 [2048], P('ctx'), may hold values from 0 to 2047, each once
- w_out: bfloat16 [8192, 4096], P(None, 'ctx'), may hold values from -0.0625 to 0.0625
Outputs:
- projected: float32 [4, 4096], P(None, 'ctx')
- log_mass: float32 [4, 64], P(None, 'kv')
Inputs may be any that keep to these rules, and one draw needn't show every extreme that they name: `lengths`: a multiple of 512; some sequence holds 262144 tokens.
All inputs are finite; a program needn't handle non-finite values.
Results may differ from a plain program's by a relative error of at most 0.003.
Values may be sent and summed in bfloat16 or wider, within the bound.
No kernel may reach another device: no remote copies, remote signals or barrier semaphores. Data moves between devices by JAX's collectives and lax.ppermute only.
A program may use at most 64 MiB of HBM per device.

v0:
```python
import math

import jax
import jax.numpy as jnp
from jax import lax
from jax.sharding import PartitionSpec as P


def shards(queries, keys, values, lengths, span_map, w_out):
    rows_total = lengths.shape[0]
    group = queries.shape[1]
    head_size = keys.shape[3]
    span_len = keys.shape[2]
    per_row = lax.axis_size("ctx") * span_map.shape[0] // rows_total
    row_index = span_map // per_row
    position = span_map % per_row
    onehot = row_index[:, None] == jnp.arange(rows_total, dtype=jnp.int32)[None, :]
    row_len = jnp.sum(jnp.where(onehot, lengths[None, :], 0), axis=1)
    live = position * span_len < row_len
    member = onehot & live[:, None]
    member_f = member.astype(jnp.float32)
    picked = jnp.einsum(
        "cr,rhd->chd", onehot.astype(jnp.bfloat16), queries, preferred_element_type=jnp.float32
    ).astype(jnp.bfloat16)
    scale = 1.0 / math.sqrt(head_size)
    scores = (
        jnp.einsum("chd,ctd->cht", picked, keys[:, 0], preferred_element_type=jnp.float32) * scale
    )
    tops = jnp.max(scores, axis=-1)
    weights = jnp.exp(scores - tops[..., None]).astype(jnp.bfloat16)
    totals = jnp.sum(weights.astype(jnp.float32), axis=-1)
    summed = jnp.einsum("cht,ctd->chd", weights, values[:, 0], preferred_element_type=jnp.float32)
    floor_value = jnp.float32(-1e30)
    tops_live = jnp.where(live[:, None], tops, floor_value)
    local_peak = jnp.max(jnp.where(member[:, :, None], tops_live[:, None, :], floor_value), axis=0)
    spread_back = jnp.einsum("cr,rh->ch", member_f, local_peak, precision=lax.Precision.HIGHEST)
    factor = jnp.exp(tops_live - spread_back)
    local_mass = jnp.einsum("cr,ch->rh", member_f, factor * totals, precision=lax.Precision.HIGHEST)
    local_out = jnp.einsum(
        "cr,chd->rhd", member_f, factor[..., None] * summed, precision=lax.Precision.HIGHEST
    )
    peak = lax.pmax(local_peak, "ctx")
    rescale = jnp.exp(local_peak - peak)
    mass, output = lax.psum((local_mass * rescale, local_out * rescale[..., None]), "ctx")
    attended = (
        (output / mass[..., None]).astype(jnp.bfloat16).reshape(rows_total, group * head_size)
    )
    log_mass = peak + jnp.log(mass)
    projected = jnp.dot(
        lax.all_gather(attended, "kv", axis=1, tiled=True),
        w_out,
        preferred_element_type=jnp.float32,
    )
    return (projected, log_mass)


def solution(mesh):
    placed = (
        P(None, "kv", None),
        P("ctx", "kv", None, None),
        P("ctx", "kv", None, None),
        P(),
        P("ctx"),
        P(None, "ctx"),
    )
    return jax.shard_map(
        shards,
        mesh=mesh,
        in_specs=placed,
        out_specs=(P(None, "ctx"), P(None, "kv")),
        check_vma=False,
    )
```

profile of v0, /device:TPU:1, one launch (start us, length us, event | category | flops | bytes accessed | tf_op | source)
XLA Modules:
  0.0 395.1 jit_solution(16237468206913726160)
XLA Ops:
  0.6 0.0 copy-start
  0.6 0.0 copy-start.2
  0.7 0.0 copy-start.1
  0.7 0.8 and_select_fusion.1
  1.4 1.0 convolution_convert_fusion
  2.4 3.5 fusion.23
  5.9 0.1 copy.21
  5.9 0.0 copy-done.1
  5.9 0.1 select_reduce_fusion.1
  6.0 0.0 copy-done.2
  6.1 0.1 select_reduce_fusion
  6.2 128.3 %pmax.7 = f32[4,16]{1,0:T(4,128)S(1)} all-reduce(f32[4,16]{1,0:T(4,128)S(1)} %select_reduce_fusion), channel_id=1, replica_groups=mesh['ctx'=64,'kv'=4] {'ctx'}, use_global_device_ids=true, to_apply=%region_3.4 | all-reduce | flops 64 | bytes 512 | tf_op jit(solution)/shard_map/pmax | solution.py:42
  134.4 0.2 fusion.10
  134.6 0.3 convert_reduce_fusion
  135.0 0.1 copy.25
  135.0 0.1 convolution_multiply_fusion.1
  135.2 0.1 copy.24
  135.2 0.1 copy.22
  135.3 2.9 fusion.7
  138.3 0.3 convolution_multiply_fusion
  138.6 245.5 %all-reduce = (f32[4,16,128]{2,0,1:T(4,128)S(1)}, f32[4,16]{1,0:T(4,128)S(1)}) all-reduce(f32[4,16,128]{2,0,1:T(4,128)S(1)} %convolution_multiply_fusion, f32[4,16]{1,0:T(4,128)S(1)} %convolution_multiply_fusion.1), channel_id=1, replica_groups=mesh['ctx'=64,'kv'=4] {'ctx'}, use_global_device_ids=true, to_apply=%region_4.5 | all-reduce | flops 8256 | bytes 66048 | tf_op jit(solution)/shard_map/psum | solution.py:44
  384.1 0.6 log_add_fusion
  384.7 0.1 copy.26
  384.7 0.1 fusion.14
  384.8 9.3 %all_gather.3 = bf16[4,8192]{1,0:T(4,128)(2,1)S(1)} all-gather(bf16[4,2048]{1,0:T(4,128)(2,1)S(1)} %fusion.14), channel_id=1, replica_groups=mesh['ctx'=64,'kv'=4] {'kv'}, dimensions={1}, use_global_device_ids=true | all-gather | bytes 81920 | tf_op jit(solution)/shard_map/all_gather | solution.py:50
  394.2 0.0 copy-done
  394.2 1.0 fusion.24
  (4 shorter events, 0.0 us)
Async XLA Ops:
  0.6 393.5 %copy-start = (bf16[8192,64]{0,1:T(8,128)(2,1)S(1)}, bf16[8192,64]{0,1:T(8,128)(2,1)}, u32[]{:S(2)}) copy-start(bf16[8192,64]{0,1:T(8,128)(2,1)} %param.11) | copy-start | bytes 3145732
  0.6 5.4 %copy-start.2 = (s32[32]{0:T(128)S(1)}, s32[32]{0:T(128)}, u32[]{:S(2)}) copy-start(s32[32]{0:T(128)} %param.10) | copy-start | bytes 388
  0.7 5.3 %copy-start.1 = (s32[4]{0:T(128)S(1)}, s32[4]{0:T(128)}, u32[]{:S(2)}) copy-start(s32[4]{0:T(128)} %param.9) | copy-start | bytes 52
where the time goes:
time: 402 us; the launch traced here: 395 us
  blocking collectives  383 us (95%)
  matrix products  8.92 us (2%)
    psum x1, blocking collectives, shards(): lax.psum((local_mass * rescale, local_out * rescale[..., None]), 'ctx')  246 us
    pmax x1, blocking collectives, shards(): peak = lax.pmax(local_peak, 'ctx')  128 us
    all_gather x1, blocking collectives, shards(): lax.all_gather(attended, 'kv', axis=1, tiled=True)  9.32 us

commit v1 on v0

v1 whole, which is shorter than its diff:
```python
import functools
import math

import jax
import jax.numpy as jnp
from jax import lax
from jax.experimental import pallas as pl
from jax.experimental.pallas import tpu as pltpu
from jax.sharding import Mesh, PartitionSpec as P

ROWS, HD, GROUP, SPAN, CPR = 4, 128, 16, 512, 512
HALF = GROUP // 2
PAIRS = ROWS * HALF
PAY = PAIRS + 8
LANES = 128
BLOCKS = LANES // PAIRS
FLOOR = -1e30
NOTHING = -32000.0
TINY = 2.0**-110
STEPS = 32760.0
SCALE = 1.0 / math.sqrt(HD)
LOG2E = math.log2(math.e)
CHUNK = 4

VMEM = pl.BlockSpec(memory_space=pltpu.VMEM)
SMEM = pl.BlockSpec(memory_space=pltpu.SMEM)
HBM = pl.BlockSpec(memory_space=pltpu.HBM)


def iota(shape, axis):
    return lax.broadcasted_iota(jnp.int32, shape, axis)


def fixed(x):
    return x.astype(jnp.int32).astype(jnp.int16)


def header(lse, power):
    whole = jnp.floor(lse)
    rest = (lse - whole) * 32768.0
    first = jnp.floor(rest)
    second = jnp.floor((rest - first) * 32768.0)
    sub = iota((8, LANES), 0)
    return jnp.where(
        sub == 0,
        whole,
        jnp.where(sub == 1, first, jnp.where(sub == 2, second, jnp.where(sub == 3, power, 0.0))),
    )


def read_headers(in_ref, members):
    tile = in_ref[members[0], PAIRS:PAY].astype(jnp.int32)
    for i in members[1:]:
        tile = tile + in_ref[i, PAIRS:PAY].astype(jnp.int32)
    tile = tile.astype(jnp.float32)
    lse = tile[0:1] + (tile[1:2] * 2.0**-15 + tile[2:3] * 2.0**-30)
    return lse, tile[3:4]


def power_of(out):
    largest = jnp.max(jnp.abs(out), axis=-1, keepdims=True)
    return jnp.ceil(jnp.log2(jnp.maximum(largest, TINY)) * 256.0 + 1.0)


def coded(out, power):
    return jnp.round(out * (jnp.exp2(power * (-1.0 / 256.0)) * STEPS))


def to_row(column, at):
    return jnp.sum(jnp.where(at, column, 0.0), axis=0, keepdims=True)


def stack(in_ref, members):
    return jnp.concatenate(
        [in_ref[i, 0:PAIRS].astype(jnp.int32).astype(jnp.float32) for i in members], axis=0
    )


def over_blocks(x, op):
    step = PAIRS
    while step < LANES:
        x = op(x, pltpu.roll(x, step, 1))
        step *= 2
    return x


def split(x):
    hi = x.astype(jnp.bfloat16)
    return hi, (x - hi.astype(jnp.float32)).astype(jnp.bfloat16)


def split_dot(weights, stacked):
    n = weights.shape[0]
    left = jnp.concatenate(split(weights), axis=0)
    right = jnp.concatenate(split(stacked), axis=1)
    four = jnp.dot(left, right, preferred_element_type=jnp.float32)
    four = four[:n] + four[n:]
    return four[:, :HD] + four[:, HD:]


def attend_kernel(
    q_ref, len_ref, map_ref, k_hbm, v_hbm, out_ref, kbuf, vbuf, qd, m_ref, l_ref, acc_ref, ksem, vsem
):
    slots = kbuf.shape[0]
    chunks = slots // CHUNK

    def copies(i):
        part = pl.ds(i * CHUNK, CHUNK)
        return (
            pltpu.make_async_copy(k_hbm.at[part], kbuf.at[part], ksem.at[i]),
            pltpu.make_async_copy(v_hbm.at[part], vbuf.at[part], vsem.at[i]),
        )

    for i in range(chunks):
        for copy in copies(i):
            copy.start()

    half_span = SPAN // 2
    qd[...] = jnp.zeros_like(qd)
    for r in range(ROWS):
        qd[r, 0:GROUP, 0:HD] = q_ref[r]
        qd[r, GROUP : 2 * GROUP, HD : 2 * HD] = q_ref[r]
    m_ref[...] = jnp.full(m_ref.shape, FLOOR, jnp.float32)
    l_ref[...] = jnp.zeros_like(l_ref)
    acc_ref[...] = jnp.zeros_like(acc_ref)
    exponent = SCALE * LOG2E

    def step(i, carry):
        kcopy, vcopy = copies(i)
        kcopy.wait()
        vcopy.wait()
        for j in range(CHUNK):
            c = i * CHUNK + j
            span = map_ref[c]
            row = lax.shift_right_logical(span, CPR.bit_length() - 1)
            position = lax.bitwise_and(span, CPR - 1)
            live = position * SPAN < len_ref[row]
            keys = jnp.concatenate([kbuf[c, 0:half_span], kbuf[c, half_span:SPAN]], axis=1)
            s = lax.dot_general(
                qd[row], keys, (((1,), (1,)), ((), ())), preferred_element_type=jnp.float32
            )
            top = jnp.max(jnp.maximum(s[:GROUP], s[GROUP:]), axis=1, keepdims=True)
            p = jnp.exp2((s - jnp.concatenate([top, top], axis=0)) * exponent).astype(jnp.bfloat16)
            pf = p.astype(jnp.float32)
            total = jnp.sum(pf[:GROUP] + pf[GROUP:], axis=1, keepdims=True)
            vals = jnp.concatenate([vbuf[c, 0:half_span], vbuf[c, half_span:SPAN]], axis=1)
            o2 = jnp.dot(p, vals, preferred_element_type=jnp.float32)
            o = o2[:GROUP, :HD] + o2[GROUP:, HD:]
            m_old = m_ref[row]
            m_new = jnp.where(live, jnp.maximum(m_old, top), m_old)
            keep = jnp.exp2((m_old - m_new) * exponent)
            add = jnp.where(live, jnp.exp2((top - m_new) * exponent), 0.0)
            m_ref[row] = m_new
            l_ref[row] = keep * l_ref[row] + add * total
            acc_ref[row] = keep * acc_ref[row] + add * o
        return carry

    lax.fori_loop(0, chunks, step, 0)

    l = l_ref[...]
    some = l > 0.0
    safe = jnp.where(some, l, 1.0)
    lse = jnp.where(some, m_ref[...] * SCALE + jnp.log(safe), NOTHING)
    out = acc_ref[...] / safe
    power = power_of(out)
    out = coded(out, power)
    block = lax.rem(lax.axis_index("z") * 2 + lax.axis_index("core"), BLOCKS)
    at = iota((PAIRS, LANES), 1) == iota((PAIRS, LANES), 0) + block * PAIRS
    for c in range(2):
        part = slice(c * HALF, (c + 1) * HALF)
        top = header(
            to_row(lse[:, part].reshape(PAIRS, LANES), at),
            to_row(power[:, part].reshape(PAIRS, 1), at),
        )
        payload = fixed(jnp.concatenate([out[:, part].reshape(PAIRS, HD), top], axis=0))
        for z in range(out_ref.shape[0] // 2):
            out_ref[2 * z + c] = payload


def merge_kernel(in_ref, out_ref):
    groups = in_ref.shape[0] // BLOCKS
    members = [[BLOCKS * j + k for k in range(BLOCKS)] for j in range(groups)]
    heads = [read_headers(in_ref, of) for of in members]
    rows = jnp.concatenate([lse for lse, _ in heads], axis=0)
    powers = jnp.concatenate([power for _, power in heads], axis=0)
    peak = over_blocks(
        jnp.broadcast_to(jnp.max(rows, axis=0, keepdims=True), (8, LANES)), jnp.maximum
    )[0:1]
    weights = jnp.exp(rows - peak)
    mass = over_blocks(
        jnp.broadcast_to(jnp.sum(weights, axis=0, keepdims=True), (8, LANES)), jnp.add
    )[0:1]
    weights = weights * jnp.exp2(powers * (1.0 / 256.0)) / (mass * STEPS)
    lse = peak + jnp.log(mass)
    pair, lane = iota((PAIRS, LANES), 0), iota((PAIRS, LANES), 1)
    spread = jnp.concatenate(
        [jnp.where(lane % PAIRS == pair, weights[j : j + 1], 0.0) for j in range(groups)], axis=1
    )
    out = split_dot(spread, jnp.concatenate([stack(in_ref, of) for of in members], axis=0))
    power = power_of(out)
    block = lax.axis_index("y")
    top = header(
        jnp.where(lane[0:1] // PAIRS == block, lse, 0.0),
        to_row(power, lane == pair + block * PAIRS),
    )
    payload = fixed(jnp.concatenate([coded(out, power), top], axis=0))
    for i in range(out_ref.shape[0]):
        out_ref[i] = payload


def project_kernel(in_ref, w_ref, proj_ref, mass_ref):
    groups = in_ref.shape[0] // BLOCKS
    members = [[groups * k + g for k in range(BLOCKS)] for g in range(groups)]
    heads = [read_headers(in_ref, of) for of in members]
    rows = jnp.concatenate([lse for lse, _ in heads], axis=0)
    powers = jnp.concatenate([power for _, power in heads], axis=0)
    peak = over_blocks(rows, jnp.maximum)
    weights = jnp.exp(rows - peak)
    mass = over_blocks(weights, jnp.add)
    weights = weights * jnp.exp2(powers * (1.0 / 256.0)) / (mass * STEPS)
    lse = peak + jnp.log(mass)
    pair = iota((PAIRS, LANES), 0)
    at = lax.rem(iota((PAIRS, LANES), 1), PAIRS) == lax.rem(pair, ROWS) * HALF + pair // ROWS
    heads = []
    for g in range(groups):
        out = split_dot(jnp.where(at, weights[g : g + 1], 0.0), stack(in_ref, members[g]))
        heads.extend(out[ROWS * h : ROWS * (h + 1)] for h in range(HALF))
    attended = jnp.concatenate(heads, axis=1).astype(jnp.bfloat16)
    proj_ref[...] = lax.dot_general(
        attended, w_ref[...], (((1,), (1,)), ((), ())), preferred_element_type=jnp.float32
    )
    sub, lane = iota((8, LANES), 0), iota((8, LANES), 1)
    result = jnp.zeros((8, LANES), jnp.float32)
    for c in range(2):
        own = jnp.sum(
            jnp.where(sub == lax.axis_index("x") * 2 + c, lse, 0.0), axis=0, keepdims=True
        )
        own = jnp.broadcast_to(own, (8, LANES))
        for r in range(ROWS):
            shifted = pltpu.roll(own, (LANES + c * HALF - r * HALF) % LANES, 1)
            result = jnp.where((sub == r) & (lane // HALF == c), shifted, result)
    mass_ref[...] = result[:ROWS, :GROUP]


def shards(queries, keys, values, lengths, span_map, w_out):
    slots = span_map.shape[0]
    z, y, x = lax.axis_size("z"), lax.axis_size("y"), lax.axis_size("x")
    f32, bf16 = jnp.float32, jnp.bfloat16
    cache = (slots, SPAN, HD)
    part = pl.pallas_call(
        attend_kernel,
        out_shape=jax.ShapeDtypeStruct((z * 2, PAY, HD), jnp.int16),
        in_specs=[VMEM, SMEM, SMEM, HBM, HBM],
        out_specs=VMEM,
        scratch_shapes=[
            pltpu.VMEM(cache, bf16),
            pltpu.VMEM(cache, bf16),
            pltpu.VMEM((ROWS, 2 * GROUP, 2 * HD), bf16),
            pltpu.VMEM((ROWS, GROUP, LANES), f32),
            pltpu.VMEM((ROWS, GROUP, LANES), f32),
            pltpu.VMEM((ROWS, GROUP, HD), f32),
            pltpu.SemaphoreType.DMA((slots // CHUNK,)),
            pltpu.SemaphoreType.DMA((slots // CHUNK,)),
        ],
        compiler_params=pltpu.CompilerParams(vmem_limit_bytes=60 * 2**20),
        name="attend",
    )(queries, lengths, span_map, keys.reshape(cache), values.reshape(cache))
    part = lax.all_to_all(part, ("z", "core"), 0, 0, tiled=True)
    part = pl.pallas_call(
        merge_kernel,
        out_shape=jax.ShapeDtypeStruct((y * x * 2, PAY, HD), jnp.int16),
        in_specs=[VMEM],
        out_specs=VMEM,
        compiler_params=pltpu.CompilerParams(vmem_limit_bytes=8 * 2**20),
        name="merge",
    )(part)
    part = lax.all_to_all(part, ("y", "x", "core"), 0, 0, tiled=True)
    return pl.pallas_call(
        project_kernel,
        out_shape=(
            jax.ShapeDtypeStruct((ROWS, w_out.shape[1]), f32),
            jax.ShapeDtypeStruct((ROWS, GROUP), f32),
        ),
        in_specs=[VMEM, VMEM],
        out_specs=(VMEM, VMEM),
        compiler_params=pltpu.CompilerParams(vmem_limit_bytes=8 * 2**20),
        name="project",
    )(part, w_out.T)


def solution(mesh):
    fine = Mesh(mesh.devices.reshape(8, 4, 2, 4), ("z", "y", "core", "x"))
    ctx = ("z", "y", "core")
    placed = (
        P(None, "x", None),
        P(ctx, "x", None, None),
        P(ctx, "x", None, None),
        P(),
        P(ctx),
        P(None, ctx),
    )
    return jax.shard_map(
        shards,
        mesh=fine,
        in_specs=placed,
        out_specs=(P(None, ctx), P(None, "x")),
        check_vma=False,
    )
```

time: 402 us -> 54 us (0.13); the launches traced: 395 us -> 53.8 us
  blocking collectives: 383 us -> 36.2 us
  Pallas kernels: 0 us -> 17 us
  matrix products: 8.92 us -> 0 us
    psum x1 -> x0, blocking collectives: 246 us -> none  [shards(): lax.psum((local_mass * rescale, local_out * rescale[..., None]), 'ctx')]
    pmax x1 -> x0, blocking collectives: 128 us -> none  [shards(): peak = lax.pmax(local_peak, 'ctx')]
    all_to_all x0 -> x2, blocking collectives: none -> 36.2 us  [the longest x1 19.6 us: shards(): part = lax.all_to_all(part, ('z', 'core'), 0, 0, tiled=True)]
    pallas_call x0 -> x3, Pallas kernels: none -> 17 us  [the longest x1 14.9 us: shards(): pl.pallas_call(attend_kernel, out_shape=jax.ShapeDtypeStruct((z * 2, PAY,...]
    all_gather x1 -> x0, blocking collectives: 9.32 us -> none  [shards(): lax.all_gather(attended, 'kv', axis=1, tiled=True)]
    dot_general x7 -> x0, matrix products: 8.92 us -> none  [the longest x1 3.46 us: shards(): jnp.einsum('chd,ctd->cht', picked, keys[:, 0], preferred_element_type=jnp...]
where the time goes in v1:
time: 54 us; the launch traced here: 53.8 us
  blocking collectives  36.2 us (67%)
  Pallas kernels  17 us (31%)
  between operations  0.66 us (1%)
    all_to_all x1, blocking collectives, shards(): part = lax.all_to_all(part, ('z', 'core'), 0, 0, tiled=True)  19.6 us
    all_to_all x1, blocking collectives, shards(): part = lax.all_to_all(part, ('y', 'x', 'core'), 0, 0, tiled=True)  16.5 us
    pallas_call x1, Pallas kernels, shards(): pl.pallas_call(attend_kernel, out_shape=jax.ShapeDtypeStruct((z * 2, PAY,...  14.9 us
    pallas_call x1, Pallas kernels, shards(): pl.pallas_call(project_kernel, out_shape=(jax.ShapeDtypeStruct((ROWS, w_o...  1.51 us

profile of v1, /device:TPU:1, one launch (start us, length us, event | category | flops | bytes accessed | tf_op | source)
XLA Modules:
  0.0 53.8 jit_solution(15484880471255636112)
XLA Ops:
  0.6 0.0 copy-start
  0.6 14.9 %attend.1 = s16[16,40,128]{2,1,0:T(8,128)(2,1)} custom-call(bf16[4,16,128]{2,1,0:T(8,128)(2,1)} %q_ref.1, s32[4]{0:T(128)} %len_ref.1, s32[32]{0:T(128)} %map_ref.1, bf16[32,512,128]{2,1,0:T(8,128)(2,1)} %bitcast.4, bf16[32,512,128]{2,1,0:T(8,128)(2,1)} %bitcast.5), custom_call_target="tpu_custom_call" | custom-call | tf_op jit(solution)/shard_map/attend/pallas_call | solution.py:250
  15.5 19.6 %all_to_all.10.in_ref = s16[16,40,128]{2,1,0:T(8,128)(2,1)S(1)} all-to-all(s16[16,40,128]{2,1,0:T(8,128)(2,1)} %attend.1), channel_id=1, replica_groups=mesh['z'=8,'y'=4,'core'=2,'x'=4] {'z','core'}, dimensions={0} | all-to-all | bytes 327680 | tf_op jit(solution)/shard_map/all_to_all | solution.py:268
  35.2 0.6 %merge.1 = s16[32,40,128]{2,1,0:T(8,128)(2,1)S(1)} custom-call(s16[16,40,128]{2,1,0:T(8,128)(2,1)S(1)} %all_to_all.10.in_ref), custom_call_target="tpu_custom_call" | custom-call | tf_op jit(solution)/shard_map/merge/pallas_call | solution.py:269
  35.8 16.5 %all_to_all.11.in_ref = s16[32,40,128]{2,1,0:T(8,128)(2,1)S(1)} all-to-all(s16[32,40,128]{2,1,0:T(8,128)(2,1)S(1)} %merge.1), channel_id=1, replica_groups=mesh['z'=8,'y'=4,'core'=2,'x'=4] {'y','x','core'}, dimensions={0} | all-to-all | bytes 655360 | tf_op jit(solution)/shard_map/all_to_all | solution.py:277
  52.3 0.0 copy-done
  52.3 1.5 %project.1 = (f32[4,64]{1,0:T(4,128)}, f32[4,16]{1,0:T(4,128)}) custom-call(s16[32,40,128]{2,1,0:T(8,128)(2,1)S(1)} %all_to_all.11.in_ref, bf16[64,8192]{1,0:T(8,128)(2,1)S(1)} %bitcast.3), custom_call_target="tpu_custom_call" | custom-call | tf_op jit(solution)/shard_map/project/pallas_call | solution.py:278
Async XLA Ops:
  0.6 51.7 %copy-start = (bf16[8192,64]{0,1:T(8,128)(2,1)S(1)}, bf16[8192,64]{0,1:T(8,128)(2,1)}, u32[]{:S(2)}) copy-start(bf16[8192,64]{0,1:T(8,128)(2,1)} %param.11) | copy-start | bytes 3145732

commit v2 on v1

--- a/solution.py
+++ b/solution.py
@@ -20,10 +20,9 @@
 STEPS = 32760.0
 SCALE = 1.0 / math.sqrt(HD)
 LOG2E = math.log2(math.e)
-CHUNK = 4
+CHUNKS = 2
 
 VMEM = pl.BlockSpec(memory_space=pltpu.VMEM)
-SMEM = pl.BlockSpec(memory_space=pltpu.SMEM)
 HBM = pl.BlockSpec(memory_space=pltpu.HBM)
 
 
@@ -99,65 +98,69 @@
 
 
 def attend_kernel(
-    q_ref, len_ref, map_ref, k_hbm, v_hbm, out_ref, kbuf, vbuf, qd, m_ref, l_ref, acc_ref, ksem, vsem
+    q_hbm, len_hbm, map_hbm, k_hbm, v_hbm, out_ref,
+    q_ref, len_ref, map_ref, kbuf, vbuf, s_ref, m_ref, l_ref, acc_ref, sem, ksem, vsem,
 ):
     slots = kbuf.shape[0]
-    chunks = slots // CHUNK
-
-    def copies(i):
-        part = pl.ds(i * CHUNK, CHUNK)
-        return (
-            pltpu.make_async_copy(k_hbm.at[part], kbuf.at[part], ksem.at[i]),
-            pltpu.make_async_copy(v_hbm.at[part], vbuf.at[part], vsem.at[i]),
+    size = slots // CHUNKS
+    parts = [pl.ds(i * size, size) for i in range(CHUNKS)]
+    small = [
+        pltpu.make_async_copy(source, target, sem.at[i])
+        for i, (source, target) in enumerate(
+            [(map_hbm, map_ref), (len_hbm, len_ref), (q_hbm, q_ref)]
         )
-
-    for i in range(chunks):
-        for copy in copies(i):
-            copy.start()
-
-    half_span = SPAN // 2
-    qd[...] = jnp.zeros_like(qd)
-    for r in range(ROWS):
-        qd[r, 0:GROUP, 0:HD] = q_ref[r]
-        qd[r, GROUP : 2 * GROUP, HD : 2 * HD] = q_ref[r]
+    ]
+    kcopies = [
+        pltpu.make_async_copy(k_hbm.at[part], kbuf.at[part], ksem.at[i])
+        for i, part in enumerate(parts)
+    ]
+    vcopies = [
+        pltpu.make_async_copy(v_hbm.at[part], vbuf.at[part], vsem.at[i])
+        for i, part in enumerate(parts)
+    ]
+    for copy in small + kcopies:
+        copy.start(priority=0)
+    for copy in vcopies:
+        copy.start(priority=1)
     m_ref[...] = jnp.full(m_ref.shape, FLOOR, jnp.float32)
     l_ref[...] = jnp.zeros_like(l_ref)
     acc_ref[...] = jnp.zeros_like(acc_ref)
-    exponent = SCALE * LOG2E
-
-    def step(i, carry):
-        kcopy, vcopy = copies(i)
-        kcopy.wait()
-        vcopy.wait()
-        for j in range(CHUNK):
-            c = i * CHUNK + j
-            span = map_ref[c]
-            row = lax.shift_right_logical(span, CPR.bit_length() - 1)
-            position = lax.bitwise_and(span, CPR - 1)
-            live = position * SPAN < len_ref[row]
-            keys = jnp.concatenate([kbuf[c, 0:half_span], kbuf[c, half_span:SPAN]], axis=1)
+    for copy in small:
+        copy.wait()
+
+    def place(c):
+        span = map_ref[c]
+        row = lax.shift_right_logical(span, CPR.bit_length() - 1)
+        return row, lax.bitwise_and(span, CPR - 1) * SPAN < len_ref[row]
+
+    def folded(x, op):
+        tiles = [x[:, i * LANES : (i + 1) * LANES] for i in range(SPAN // LANES)]
+        return op(op(tiles[0], tiles[1]), op(tiles[2], tiles[3]))
+
+    for i, copy in enumerate(kcopies):
+        copy.wait()
+        for c in range(i * size, (i + 1) * size):
+            row, live = place(c)
             s = lax.dot_general(
-                qd[row], keys, (((1,), (1,)), ((), ())), preferred_element_type=jnp.float32
+                q_ref[row], kbuf[c], (((1,), (1,)), ((), ())), preferred_element_type=jnp.float32
             )
-            top = jnp.max(jnp.maximum(s[:GROUP], s[GROUP:]), axis=1, keepdims=True)
-            p = jnp.exp2((s - jnp.concatenate([top, top], axis=0)) * exponent).astype(jnp.bfloat16)
-            pf = p.astype(jnp.float32)
-            total = jnp.sum(pf[:GROUP] + pf[GROUP:], axis=1, keepdims=True)
-            vals = jnp.concatenate([vbuf[c, 0:half_span], vbuf[c, half_span:SPAN]], axis=1)
-            o2 = jnp.dot(p, vals, preferred_element_type=jnp.float32)
-            o = o2[:GROUP, :HD] + o2[GROUP:, HD:]
-            m_old = m_ref[row]
-            m_new = jnp.where(live, jnp.maximum(m_old, top), m_old)
-            keep = jnp.exp2((m_old - m_new) * exponent)
-            add = jnp.where(live, jnp.exp2((top - m_new) * exponent), 0.0)
-            m_ref[row] = m_new
-            l_ref[row] = keep * l_ref[row] + add * total
-            acc_ref[row] = keep * acc_ref[row] + add * o
-        return carry
-
-    lax.fori_loop(0, chunks, step, 0)
-
-    l = l_ref[...]
+            s_ref[c] = s
+            m_ref[row] = jnp.maximum(
+                m_ref[row], jnp.where(live, folded(s, jnp.maximum), FLOOR)
+            )
+    m_ref[...] = jnp.broadcast_to(jnp.max(m_ref[...], axis=2, keepdims=True), m_ref.shape)
+
+    for i, copy in enumerate(vcopies):
+        copy.wait()
+        for c in range(i * size, (i + 1) * size):
+            row, live = place(c)
+            top = jnp.where(live, m_ref[row], -FLOOR)
+            top = jnp.concatenate([top] * (SPAN // LANES), axis=1)
+            p = jnp.exp2((s_ref[c] - top) * (SCALE * LOG2E)).astype(jnp.bfloat16)
+            l_ref[row] += folded(p.astype(jnp.float32), jnp.add)
+            acc_ref[row] += jnp.dot(p, vbuf[c], preferred_element_type=jnp.float32)
+
+    l = jnp.broadcast_to(jnp.sum(l_ref[...], axis=2, keepdims=True), l_ref.shape)
     some = l > 0.0
     safe = jnp.where(some, l, 1.0)
     lse = jnp.where(some, m_ref[...] * SCALE + jnp.log(safe), NOTHING)
@@ -250,17 +253,21 @@
     part = pl.pallas_call(
         attend_kernel,
         out_shape=jax.ShapeDtypeStruct((z * 2, PAY, HD), jnp.int16),
-        in_specs=[VMEM, SMEM, SMEM, HBM, HBM],
+        in_specs=[HBM] * 5,
         out_specs=VMEM,
         scratch_shapes=[
+            pltpu.VMEM((ROWS, GROUP, HD), bf16),
+            pltpu.SMEM((ROWS,), jnp.int32),
+            pltpu.SMEM((slots,), jnp.int32),
             pltpu.VMEM(cache, bf16),
             pltpu.VMEM(cache, bf16),
-            pltpu.VMEM((ROWS, 2 * GROUP, 2 * HD), bf16),
+            pltpu.VMEM((slots, GROUP, SPAN), f32),
             pltpu.VMEM((ROWS, GROUP, LANES), f32),
             pltpu.VMEM((ROWS, GROUP, LANES), f32),
             pltpu.VMEM((ROWS, GROUP, HD), f32),
-            pltpu.SemaphoreType.DMA((slots // CHUNK,)),
-            pltpu.SemaphoreType.DMA((slots // CHUNK,)),
+            pltpu.SemaphoreType.DMA((3,)),
+            pltpu.SemaphoreType.DMA((CHUNKS,)),
+            pltpu.SemaphoreType.DMA((CHUNKS,)),
         ],
         compiler_params=pltpu.CompilerParams(vmem_limit_bytes=60 * 2**20),
         name="attend",

time: 54 us -> 44 us (0.81)
  Pallas kernels: 17 us -> 6.96 us
    pallas_call x1, Pallas kernels: 14.9 us -> 4.86 us  [shards(): pl.pallas_call(attend_kernel, out_shape=jax.ShapeDtypeStruct((z * 2, PAY,...]
where the time goes in v2:
time: 44 us; the launch traced here: 43.8 us
  blocking collectives  36.2 us (82%)
  Pallas kernels  6.96 us (16%)
  between operations  0.66 us (2%)
    all_to_all x1, blocking collectives, shards(): part = lax.all_to_all(part, ('z', 'core'), 0, 0, tiled=True)  19.6 us
    all_to_all x1, blocking collectives, shards(): part = lax.all_to_all(part, ('y', 'x', 'core'), 0, 0, tiled=True)  16.5 us
    pallas_call x1, Pallas kernels, shards(): pl.pallas_call(attend_kernel, out_shape=jax.ShapeDtypeStruct((z * 2, PAY,...  4.86 us
    pallas_call x1, Pallas kernels, shards(): pl.pallas_call(project_kernel, out_shape=(jax.ShapeDtypeStruct((ROWS, w_o...  1.51 us

profile of v2, /device:TPU:1, one launch (start us, length us, event | category | flops | bytes accessed | tf_op | source)
XLA Modules:
  0.0 43.8 jit_solution(9620559879345367851)
XLA Ops:
  0.6 0.0 copy-start
  0.6 4.9 %attend.1 = s16[16,40,128]{2,1,0:T(8,128)(2,1)} custom-call(bf16[4,16,128]{2,1,0:T(8,128)(2,1)} %q_hbm.1, s32[4]{0:T(128)} %len_hbm.1, s32[32]{0:T(128)} %map_hbm.1, bf16[32,512,128]{2,1,0:T(8,128)(2,1)} %bitcast.4, bf16[32,512,128]{2,1,0:T(8,128)(2,1)} %bitcast.5), custom_call_target="tpu_custom_call" | custom-call | tf_op jit(solution)/shard_map/attend/pallas_call | solution.py:253
  5.5 19.6 %all_to_all.10.in_ref = s16[16,40,128]{2,1,0:T(8,128)(2,1)S(1)} all-to-all(s16[16,40,128]{2,1,0:T(8,128)(2,1)} %attend.1), channel_id=1, replica_groups=mesh['z'=8,'y'=4,'core'=2,'x'=4] {'z','core'}, dimensions={0} | all-to-all | bytes 327680 | tf_op jit(solution)/shard_map/all_to_all | solution.py:275
  25.1 0.6 %merge.1 = s16[32,40,128]{2,1,0:T(8,128)(2,1)S(1)} custom-call(s16[16,40,128]{2,1,0:T(8,128)(2,1)S(1)} %all_to_all.10.in_ref), custom_call_target="tpu_custom_call" | custom-call | tf_op jit(solution)/shard_map/merge/pallas_call | solution.py:276
  25.7 16.5 %all_to_all.11.in_ref = s16[32,40,128]{2,1,0:T(8,128)(2,1)S(1)} all-to-all(s16[32,40,128]{2,1,0:T(8,128)(2,1)S(1)} %merge.1), channel_id=1, replica_groups=mesh['z'=8,'y'=4,'core'=2,'x'=4] {'y','x','core'}, dimensions={0} | all-to-all | bytes 655360 | tf_op jit(solution)/shard_map/all_to_all | solution.py:284
  42.3 0.0 copy-done
  42.3 1.5 %project.1 = (f32[4,64]{1,0:T(4,128)}, f32[4,16]{1,0:T(4,128)}) custom-call(s16[32,40,128]{2,1,0:T(8,128)(2,1)S(1)} %all_to_all.11.in_ref, bf16[64,8192]{1,0:T(8,128)(2,1)S(1)} %bitcast.3), custom_call_target="tpu_custom_call" | custom-call | tf_op jit(solution)/shard_map/project/pallas_call | solution.py:285
Async XLA Ops:
  0.6 41.6 %copy-start = (bf16[8192,64]{0,1:T(8,128)(2,1)S(1)}, bf16[8192,64]{0,1:T(8,128)(2,1)}, u32[]{:S(2)}) copy-start(bf16[8192,64]{0,1:T(8,128)(2,1)} %param.11) | copy-start | bytes 3145732

commit v3 on v2

--- a/solution.py
+++ b/solution.py
@@ -11,7 +11,7 @@
 ROWS, HD, GROUP, SPAN, CPR = 4, 128, 16, 512, 512
 HALF = GROUP // 2
 PAIRS = ROWS * HALF
-PAY = PAIRS + 8
+PAY = PAIRS + 2
 LANES = 128
 BLOCKS = LANES // PAIRS
 FLOOR = -1e30
@@ -39,21 +39,32 @@
     rest = (lse - whole) * 32768.0
     first = jnp.floor(rest)
     second = jnp.floor((rest - first) * 32768.0)
-    sub = iota((8, LANES), 0)
-    return jnp.where(
-        sub == 0,
-        whole,
-        jnp.where(sub == 1, first, jnp.where(sub == 2, second, jnp.where(sub == 3, power, 0.0))),
-    )
-
-
-def read_headers(in_ref, members):
-    tile = in_ref[members[0], PAIRS:PAY].astype(jnp.int32)
-    for i in members[1:]:
-        tile = tile + in_ref[i, PAIRS:PAY].astype(jnp.int32)
-    tile = tile.astype(jnp.float32)
-    lse = tile[0:1] + (tile[1:2] * 2.0**-15 + tile[2:3] * 2.0**-30)
-    return lse, tile[3:4]
+    shape = (PAIRS, LANES)
+    block = iota(shape, 1) // PAIRS
+    kind = jnp.where(block == 0, whole, jnp.where(block == 1, first, second))
+    kind = jnp.where(block == 3, power, kind)
+    row = jnp.sum(
+        jnp.where(iota(shape, 1) % PAIRS == iota(shape, 0), kind, 0.0), axis=0, keepdims=True
+    )
+    return jnp.broadcast_to(row, (2, LANES))
+
+
+def read_headers(flat, members):
+    rows = [flat[i, PAIRS:PAY].astype(jnp.int32).astype(jnp.float32)[0:1] for i in members]
+    rows = jnp.concatenate(rows, axis=0)
+    block = iota(rows.shape, 1) // PAIRS
+    unit = jnp.where(block == 0, 1.0, jnp.where(block == 1, 2.0**-15, 2.0**-30))
+    lse = over_blocks(jnp.where(block == 3, 0.0, rows * unit), jnp.add)
+    scale = over_blocks(jnp.where(block == 3, rows, 0.0), jnp.add)
+    return lse, jnp.exp2(scale * (1.0 / 256.0)) * (1.0 / STEPS)
+
+
+def by_block(tiles):
+    block = iota(tiles[0].shape, 1) // PAIRS
+    out = tiles[0]
+    for k in range(1, BLOCKS):
+        out = jnp.where(block == k, tiles[k], out)
+    return out
 
 
 def power_of(out):
@@ -65,13 +76,9 @@
     return jnp.round(out * (jnp.exp2(power * (-1.0 / 256.0)) * STEPS))
 
 
-def to_row(column, at):
-    return jnp.sum(jnp.where(at, column, 0.0), axis=0, keepdims=True)
-
-
-def stack(in_ref, members):
+def stack(flat, members):
     return jnp.concatenate(
-        [in_ref[i, 0:PAIRS].astype(jnp.int32).astype(jnp.float32) for i in members], axis=0
+        [flat[i, 0:PAIRS].astype(jnp.int32).astype(jnp.float32) for i in members], axis=0
     )
 
 
@@ -167,66 +174,53 @@
     out = acc_ref[...] / safe
     power = power_of(out)
     out = coded(out, power)
-    block = lax.rem(lax.axis_index("z") * 2 + lax.axis_index("core"), BLOCKS)
-    at = iota((PAIRS, LANES), 1) == iota((PAIRS, LANES), 0) + block * PAIRS
+    flat = out_ref.reshape(out_ref.shape[0], PAY, HD)
     for c in range(2):
         part = slice(c * HALF, (c + 1) * HALF)
-        top = header(
-            to_row(lse[:, part].reshape(PAIRS, LANES), at),
-            to_row(power[:, part].reshape(PAIRS, 1), at),
-        )
+        top = header(lse[:, part].reshape(PAIRS, LANES), power[:, part].reshape(PAIRS, 1))
         payload = fixed(jnp.concatenate([out[:, part].reshape(PAIRS, HD), top], axis=0))
         for z in range(out_ref.shape[0] // 2):
-            out_ref[2 * z + c] = payload
+            flat[2 * z + c] = payload
 
 
 def merge_kernel(in_ref, out_ref):
+    flat = in_ref.reshape(in_ref.shape[0], PAY, HD)
+    halves = [range(0, 8), range(8, 16)]
+    heads = [read_headers(flat, half) for half in halves]
+    peak = jnp.max(jnp.maximum(heads[0][0], heads[1][0]), axis=0, keepdims=True)
+    weights = [jnp.exp(lse - peak) for lse, _ in heads]
+    mass = jnp.sum(weights[0] + weights[1], axis=0, keepdims=True)
+    lse = peak + jnp.log(mass)
+    weights = [w * scale / mass for w, (_, scale) in zip(weights, heads)]
+    groups = BLOCKS
+    rows = by_block([t for w in weights for t in (w, pltpu.roll(w, 4, 0))])
+    at = iota((PAIRS, LANES), 1) % PAIRS == iota((PAIRS, LANES), 0)
+    spread = jnp.concatenate(
+        [jnp.where(at, rows[g : g + 1], 0.0) for g in range(groups)], axis=1
+    )
+    members = [k * groups + g for g in range(groups) for k in range(BLOCKS)]
+    out = split_dot(spread, stack(flat, members))
+    power = power_of(out)
+    payload = fixed(jnp.concatenate([coded(out, power), header(lse, power)], axis=0))
+    sent = out_ref.reshape(out_ref.shape[0], PAY, HD)
+    for i in range(out_ref.shape[0]):
+        sent[i] = payload
+
+
+def project_kernel(in_ref, w_ref, proj_ref, mass_ref):
+    flat = in_ref.reshape(in_ref.shape[0], PAY, HD)
     groups = in_ref.shape[0] // BLOCKS
-    members = [[BLOCKS * j + k for k in range(BLOCKS)] for j in range(groups)]
-    heads = [read_headers(in_ref, of) for of in members]
-    rows = jnp.concatenate([lse for lse, _ in heads], axis=0)
-    powers = jnp.concatenate([power for _, power in heads], axis=0)
-    peak = over_blocks(
-        jnp.broadcast_to(jnp.max(rows, axis=0, keepdims=True), (8, LANES)), jnp.maximum
-    )[0:1]
-    weights = jnp.exp(rows - peak)
-    mass = over_blocks(
-        jnp.broadcast_to(jnp.sum(weights, axis=0, keepdims=True), (8, LANES)), jnp.add
-    )[0:1]
-    weights = weights * jnp.exp2(powers * (1.0 / 256.0)) / (mass * STEPS)
+    heads = [read_headers(flat, range(groups * y, groups * (y + 1))) for y in range(BLOCKS)]
+    peak = functools.reduce(jnp.maximum, [lse for lse, _ in heads])
+    weights = [jnp.exp(lse - peak) for lse, _ in heads]
+    mass = functools.reduce(jnp.add, weights)
     lse = peak + jnp.log(mass)
-    pair, lane = iota((PAIRS, LANES), 0), iota((PAIRS, LANES), 1)
-    spread = jnp.concatenate(
-        [jnp.where(lane % PAIRS == pair, weights[j : j + 1], 0.0) for j in range(groups)], axis=1
-    )
-    out = split_dot(spread, jnp.concatenate([stack(in_ref, of) for of in members], axis=0))
-    power = power_of(out)
-    block = lax.axis_index("y")
-    top = header(
-        jnp.where(lane[0:1] // PAIRS == block, lse, 0.0),
-        to_row(power, lane == pair + block * PAIRS),
-    )
-    payload = fixed(jnp.concatenate([coded(out, power), top], axis=0))
-    for i in range(out_ref.shape[0]):
-        out_ref[i] = payload
-
-
-def project_kernel(in_ref, w_ref, proj_ref, mass_ref):
-    groups = in_ref.shape[0] // BLOCKS
-    members = [[groups * k + g for k in range(BLOCKS)] for g in range(groups)]
-    heads = [read_headers(in_ref, of) for of in members]
-    rows = jnp.concatenate([lse for lse, _ in heads], axis=0)
-    powers = jnp.concatenate([power for _, power in heads], axis=0)
-    peak = over_blocks(rows, jnp.maximum)
-    weights = jnp.exp(rows - peak)
-    mass = over_blocks(weights, jnp.add)
-    weights = weights * jnp.exp2(powers * (1.0 / 256.0)) / (mass * STEPS)
-    lse = peak + jnp.log(mass)
+    weights = by_block([w * scale / mass for w, (_, scale) in zip(weights, heads)])
     pair = iota((PAIRS, LANES), 0)
     at = lax.rem(iota((PAIRS, LANES), 1), PAIRS) == lax.rem(pair, ROWS) * HALF + pair // ROWS
     heads = []
     for g in range(groups):
-        out = split_dot(jnp.where(at, weights[g : g + 1], 0.0), stack(in_ref, members[g]))
+        out = split_dot(jnp.where(at, weights[g : g + 1], 0.0), stack(flat, [groups * y + g for y in range(BLOCKS)]))
         heads.extend(out[ROWS * h : ROWS * (h + 1)] for h in range(HALF))
     attended = jnp.concatenate(heads, axis=1).astype(jnp.bfloat16)
     proj_ref[...] = lax.dot_general(
@@ -252,7 +246,7 @@
     cache = (slots, SPAN, HD)
     part = pl.pallas_call(
         attend_kernel,
-        out_shape=jax.ShapeDtypeStruct((z * 2, PAY, HD), jnp.int16),
+        out_shape=jax.ShapeDtypeStruct((z * 2, PAY // 2, 2, HD), jnp.int16),
         in_specs=[HBM] * 5,
         out_specs=VMEM,
         scratch_shapes=[
@@ -275,7 +269,7 @@
     part = lax.all_to_all(part, ("z", "core"), 0, 0, tiled=True)
     part = pl.pallas_call(
         merge_kernel,
-        out_shape=jax.ShapeDtypeStruct((y * x * 2, PAY, HD), jnp.int16),
+        out_shape=jax.ShapeDtypeStruct((y * x * 2, PAY // 2, 2, HD), jnp.int16),
         in_specs=[VMEM],
         out_specs=VMEM,
         compiler_params=pltpu.CompilerParams(vmem_limit_bytes=8 * 2**20),

time: 44 us -> 43.2 us (0.982)
  blocking collectives: 36.2 us -> 35.4 us
    all_to_all x1, blocking collectives: 16.5 us -> 16.1 us  [shards(): part = lax.all_to_all(part, ('y', 'x', 'core'), 0, 0, tiled=True)]
where the time goes in v3:
time: 43.2 us; the launch traced here: 43 us
  blocking collectives  35.4 us (82%)
  Pallas kernels  6.95 us (16%)
  between operations  0.66 us (2%)
    all_to_all x1, blocking collectives, shards(): part = lax.all_to_all(part, ('z', 'core'), 0, 0, tiled=True)  19.3 us
    all_to_all x1, blocking collectives, shards(): part = lax.all_to_all(part, ('y', 'x', 'core'), 0, 0, tiled=True)  16.1 us
    pallas_call x1, Pallas kernels, shards(): pl.pallas_call(attend_kernel, out_shape=jax.ShapeDtypeStruct((z * 2, PAY...  4.9 us
    pallas_call x1, Pallas kernels, shards(): pl.pallas_call(project_kernel, out_shape=(jax.ShapeDtypeStruct((ROWS, w_o...  1.44 us

profile of v3, /device:TPU:1, one launch (start us, length us, event | category | flops | bytes accessed | tf_op | source)
XLA Modules:
  0.0 43.0 jit_solution(11232507052001033944)
XLA Ops:
  0.6 0.0 copy-start
  0.6 4.9 %attend.1 = s16[16,17,2,128]{3,2,1,0:T(2,128)(2,1)} custom-call(bf16[4,16,128]{2,1,0:T(8,128)(2,1)} %q_hbm.1, s32[4]{0:T(128)} %len_hbm.1, s32[32]{0:T(128)} %map_hbm.1, bf16[32,512,128]{2,1,0:T(8,128)(2,1)} %bitcast.4, bf16[32,512,128]{2,1,0:T(8,128)(2,1)} %bitcast.5), custom_call_target="tpu_custom_call" | custom-call | tf_op jit(solution)/shard_map/attend/pallas_call | solution.py:247
  5.6 19.3 %all_to_all.10.in_ref = s16[16,17,2,128]{3,2,1,0:T(2,128)(2,1)S(1)} all-to-all(s16[16,17,2,128]{3,2,1,0:T(2,128)(2,1)} %attend.1), channel_id=1, replica_groups=mesh['z'=8,'y'=4,'core'=2,'x'=4] {'z','core'}, dimensions={0} | all-to-all | bytes 278528 | tf_op jit(solution)/shard_map/all_to_all | solution.py:269
  24.9 0.6 %merge.1 = s16[32,17,2,128]{3,2,1,0:T(2,128)(2,1)S(1)} custom-call(s16[16,17,2,128]{3,2,1,0:T(2,128)(2,1)S(1)} %all_to_all.10.in_ref), custom_call_target="tpu_custom_call" | custom-call | tf_op jit(solution)/shard_map/merge/pallas_call | solution.py:270
  25.5 16.1 %all_to_all.11.in_ref = s16[32,17,2,128]{3,2,1,0:T(2,128)(2,1)S(1)} all-to-all(s16[32,17,2,128]{3,2,1,0:T(2,128)(2,1)S(1)} %merge.1), channel_id=1, replica_groups=mesh['z'=8,'y'=4,'core'=2,'x'=4] {'y','x','core'}, dimensions={0} | all-to-all | bytes 557056 | tf_op jit(solution)/shard_map/all_to_all | solution.py:278
  41.5 0.0 copy-done
  41.6 1.4 %project.1 = (f32[4,64]{1,0:T(4,128)}, f32[4,16]{1,0:T(4,128)}) custom-call(s16[32,17,2,128]{3,2,1,0:T(2,128)(2,1)S(1)} %all_to_all.11.in_ref, bf16[64,8192]{1,0:T(8,128)(2,1)S(1)} %bitcast.3), custom_call_target="tpu_custom_call" | custom-call | tf_op jit(solution)/shard_map/project/pallas_call | solution.py:279
Async XLA Ops:
  0.6 40.9 %copy-start = (bf16[8192,64]{0,1:T(8,128)(2,1)S(1)}, bf16[8192,64]{0,1:T(8,128)(2,1)}, u32[]{:S(2)}) copy-start(bf16[8192,64]{0,1:T(8,128)(2,1)} %param.11) | copy-start | bytes 3145732

commit v4 on v3

--- a/solution.py
+++ b/solution.py
@@ -20,7 +20,8 @@
 STEPS = 32760.0
 SCALE = 1.0 / math.sqrt(HD)
 LOG2E = math.log2(math.e)
-CHUNKS = 2
+KEY_PARTS = (16, 16)
+VALUE_PARTS = (16, 16)
 
 VMEM = pl.BlockSpec(memory_space=pltpu.VMEM)
 HBM = pl.BlockSpec(memory_space=pltpu.HBM)
@@ -108,23 +109,24 @@
     q_hbm, len_hbm, map_hbm, k_hbm, v_hbm, out_ref,
     q_ref, len_ref, map_ref, kbuf, vbuf, s_ref, m_ref, l_ref, acc_ref, sem, ksem, vsem,
 ):
-    slots = kbuf.shape[0]
-    size = slots // CHUNKS
-    parts = [pl.ds(i * size, size) for i in range(CHUNKS)]
     small = [
         pltpu.make_async_copy(source, target, sem.at[i])
         for i, (source, target) in enumerate(
             [(map_hbm, map_ref), (len_hbm, len_ref), (q_hbm, q_ref)]
         )
     ]
-    kcopies = [
-        pltpu.make_async_copy(k_hbm.at[part], kbuf.at[part], ksem.at[i])
-        for i, part in enumerate(parts)
-    ]
-    vcopies = [
-        pltpu.make_async_copy(v_hbm.at[part], vbuf.at[part], vsem.at[i])
-        for i, part in enumerate(parts)
-    ]
+
+    def copies(source, target, sems, sizes):
+        at = [sum(sizes[:i]) for i in range(len(sizes))]
+        return [range(start, start + size) for start, size in zip(at, sizes)], [
+            pltpu.make_async_copy(
+                source.at[pl.ds(start, size)], target.at[pl.ds(start, size)], sems.at[i]
+            )
+            for i, (start, size) in enumerate(zip(at, sizes))
+        ]
+
+    kparts, kcopies = copies(k_hbm, kbuf, ksem, KEY_PARTS)
+    vparts, vcopies = copies(v_hbm, vbuf, vsem, VALUE_PARTS)
     for copy in small + kcopies:
         copy.start(priority=0)
     for copy in vcopies:
@@ -144,9 +146,9 @@
         tiles = [x[:, i * LANES : (i + 1) * LANES] for i in range(SPAN // LANES)]
         return op(op(tiles[0], tiles[1]), op(tiles[2], tiles[3]))
 
-    for i, copy in enumerate(kcopies):
+    for part, copy in zip(kparts, kcopies):
         copy.wait()
-        for c in range(i * size, (i + 1) * size):
+        for c in part:
             row, live = place(c)
             s = lax.dot_general(
                 q_ref[row], kbuf[c], (((1,), (1,)), ((), ())), preferred_element_type=jnp.float32
@@ -157,9 +159,9 @@
             )
     m_ref[...] = jnp.broadcast_to(jnp.max(m_ref[...], axis=2, keepdims=True), m_ref.shape)
 
-    for i, copy in enumerate(vcopies):
+    for part, copy in zip(vparts, vcopies):
         copy.wait()
-        for c in range(i * size, (i + 1) * size):
+        for c in part:
             row, live = place(c)
             top = jnp.where(live, m_ref[row], -FLOOR)
             top = jnp.concatenate([top] * (SPAN // LANES), axis=1)
@@ -244,9 +246,11 @@
     z, y, x = lax.axis_size("z"), lax.axis_size("y"), lax.axis_size("x")
     f32, bf16 = jnp.float32, jnp.bfloat16
     cache = (slots, SPAN, HD)
+    inputs = (queries, lengths, span_map, keys.reshape(cache), values.reshape(cache))
+    inputs = [pltpu.with_memory_space_constraint(x, pltpu.HBM) for x in inputs]
     part = pl.pallas_call(
         attend_kernel,
-        out_shape=jax.ShapeDtypeStruct((z * 2, PAY // 2, 2, HD), jnp.int16),
+        out_shape=pltpu.VMEM((z * 2, PAY // 2, 2, HD), jnp.int16),
         in_specs=[HBM] * 5,
         out_specs=VMEM,
         scratch_shapes=[
@@ -260,12 +264,12 @@
             pltpu.VMEM((ROWS, GROUP, LANES), f32),
             pltpu.VMEM((ROWS, GROUP, HD), f32),
             pltpu.SemaphoreType.DMA((3,)),
-            pltpu.SemaphoreType.DMA((CHUNKS,)),
-            pltpu.SemaphoreType.DMA((CHUNKS,)),
+            pltpu.SemaphoreType.DMA((len(KEY_PARTS),)),
+            pltpu.SemaphoreType.DMA((len(VALUE_PARTS),)),
         ],
-        compiler_params=pltpu.CompilerParams(vmem_limit_bytes=60 * 2**20),
+        compiler_params=pltpu.CompilerParams(vmem_limit_bytes=24 * 2**20),
         name="attend",
-    )(queries, lengths, span_map, keys.reshape(cache), values.reshape(cache))
+    )(*inputs)
     part = lax.all_to_all(part, ("z", "core"), 0, 0, tiled=True)
     part = pl.pallas_call(
         merge_kernel,

time: 43.2 us -> 42.3 us (0.979)
  Pallas kernels: 6.95 us -> 6.3 us
    pallas_call x1, Pallas kernels: 4.9 us -> 4.26 us  [shards(): pl.pallas_call(attend_kernel, out_shape=pltpu.VMEM((z * 2, PAY // 2, 2, H...]
where the time goes in v4:
time: 42.3 us; the launch traced here: 42.1 us
  blocking collectives  35.2 us (83%)
  Pallas kernels  6.3 us (15%)
  between operations  0.66 us (2%)
    all_to_all x1, blocking collectives, shards(): part = lax.all_to_all(part, ('z', 'core'), 0, 0, tiled=True)  19.1 us
    all_to_all x1, blocking collectives, shards(): part = lax.all_to_all(part, ('y', 'x', 'core'), 0, 0, tiled=True)  16.1 us
    pallas_call x1, Pallas kernels, shards(): pl.pallas_call(attend_kernel, out_shape=pltpu.VMEM((z * 2, PAY // 2, 2, H...  4.26 us
    pallas_call x1, Pallas kernels, shards(): pl.pallas_call(project_kernel, out_shape=(jax.ShapeDtypeStruct((ROWS, w_o...  1.44 us

profile of v4, /device:TPU:1, one launch (start us, length us, event | category | flops | bytes accessed | tf_op | source)
XLA Modules:
  0.0 42.1 jit_solution(2118904537104391201)
XLA Ops:
  0.6 0.0 copy-start
  0.6 4.3 %attend.1 = s16[16,17,2,128]{3,2,1,0:T(2,128)(2,1)S(1)} custom-call(bf16[4,16,128]{2,1,0:T(8,128)(2,1)} %q_hbm.1, s32[4]{0:T(128)} %len_hbm.1, s32[32]{0:T(128)} %map_hbm.1, bf16[32,512,128]{2,1,0:T(8,128)(2,1)} %bitcast.4, bf16[32,512,128]{2,1,0:T(8,128)(2,1)} %bitcast.5), custom_call_target="tpu_custom_call" | custom-call | tf_op jit(solution)/shard_map/attend/pallas_call | solution.py:251
  4.9 19.1 %all_to_all.10.in_ref = s16[16,17,2,128]{3,2,1,0:T(2,128)(2,1)S(1)} all-to-all(s16[16,17,2,128]{3,2,1,0:T(2,128)(2,1)S(1)} %attend.1), channel_id=1, replica_groups=mesh['z'=8,'y'=4,'core'=2,'x'=4] {'z','core'}, dimensions={0} | all-to-all | bytes 278528 | tf_op jit(solution)/shard_map/all_to_all | solution.py:273
  24.0 0.6 %merge.1 = s16[32,17,2,128]{3,2,1,0:T(2,128)(2,1)S(1)} custom-call(s16[16,17,2,128]{3,2,1,0:T(2,128)(2,1)S(1)} %all_to_all.10.in_ref), custom_call_target="tpu_custom_call" | custom-call | tf_op jit(solution)/shard_map/merge/pallas_call | solution.py:274
  24.6 16.1 %all_to_all.11.in_ref = s16[32,17,2,128]{3,2,1,0:T(2,128)(2,1)S(1)} all-to-all(s16[32,17,2,128]{3,2,1,0:T(2,128)(2,1)S(1)} %merge.1), channel_id=1, replica_groups=mesh['z'=8,'y'=4,'core'=2,'x'=4] {'y','x','core'}, dimensions={0} | all-to-all | bytes 557056 | tf_op jit(solution)/shard_map/all_to_all | solution.py:282
  40.7 0.0 copy-done
  40.7 1.4 %project.1 = (f32[4,64]{1,0:T(4,128)}, f32[4,16]{1,0:T(4,128)}) custom-call(s16[32,17,2,128]{3,2,1,0:T(2,128)(2,1)S(1)} %all_to_all.11.in_ref, bf16[64,8192]{1,0:T(8,128)(2,1)S(1)} %bitcast.3), custom_call_target="tpu_custom_call" | custom-call | tf_op jit(solution)/shard_map/project/pallas_call | solution.py:283
Async XLA Ops:
  0.6 40.1 %copy-start = (bf16[8192,64]{0,1:T(8,128)(2,1)S(1)}, bf16[8192,64]{0,1:T(8,128)(2,1)}, u32[]{:S(2)}) copy-start(bf16[8192,64]{0,1:T(8,128)(2,1)} %param.11) | copy-start | bytes 3145732

commit v5 on v4

--- a/solution.py
+++ b/solution.py
@@ -77,10 +77,15 @@
     return jnp.round(out * (jnp.exp2(power * (-1.0 / 256.0)) * STEPS))
 
 
-def stack(flat, members):
-    return jnp.concatenate(
-        [flat[i, 0:PAIRS].astype(jnp.int32).astype(jnp.float32) for i in members], axis=0
-    )
+def weighted_sum(flat, row, members):
+    shape = (PAIRS, LANES)
+    block = iota(shape, 1) // PAIRS
+    spread = jnp.where(iota(shape, 1) % PAIRS == iota(shape, 0), row, 0.0)
+    terms = []
+    for k, i in enumerate(members):
+        column = jnp.sum(jnp.where(block == k, spread, 0.0), axis=1, keepdims=True)
+        terms.append(column * flat[i, 0:PAIRS].astype(jnp.int32).astype(jnp.float32))
+    return (terms[0] + terms[1]) + (terms[2] + terms[3])
 
 
 def over_blocks(x, op):
@@ -91,23 +96,9 @@
     return x
 
 
-def split(x):
-    hi = x.astype(jnp.bfloat16)
-    return hi, (x - hi.astype(jnp.float32)).astype(jnp.bfloat16)
-
-
-def split_dot(weights, stacked):
-    n = weights.shape[0]
-    left = jnp.concatenate(split(weights), axis=0)
-    right = jnp.concatenate(split(stacked), axis=1)
-    four = jnp.dot(left, right, preferred_element_type=jnp.float32)
-    four = four[:n] + four[n:]
-    return four[:, :HD] + four[:, HD:]
-
-
 def attend_kernel(
     q_hbm, len_hbm, map_hbm, k_hbm, v_hbm, out_ref,
-    q_ref, len_ref, map_ref, kbuf, vbuf, s_ref, m_ref, l_ref, acc_ref, sem, ksem, vsem,
+    q_ref, len_ref, map_ref, kbuf, vbuf, s_ref, m_ref, l_ref, acc_ref, order, sem, ksem, vsem,
 ):
     small = [
         pltpu.make_async_copy(source, target, sem.at[i])
@@ -178,9 +169,11 @@
     out = coded(out, power)
     flat = out_ref.reshape(out_ref.shape[0], PAY, HD)
     for c in range(2):
-        part = slice(c * HALF, (c + 1) * HALF)
-        top = header(lse[:, part].reshape(PAIRS, LANES), power[:, part].reshape(PAIRS, 1))
-        payload = fixed(jnp.concatenate([out[:, part].reshape(PAIRS, HD), top], axis=0))
+        for i, values in enumerate((out, lse, jnp.broadcast_to(power, out.shape))):
+            for r in range(ROWS):
+                order[c, i, pl.ds(r, HALF, stride=ROWS), :] = values[r, c * HALF : (c + 1) * HALF]
+        payload = jnp.concatenate([order[c, 0], header(order[c, 1], order[c, 2])], axis=0)
+        payload = fixed(payload)
         for z in range(out_ref.shape[0] // 2):
             flat[2 * z + c] = payload
 
@@ -196,12 +189,11 @@
     weights = [w * scale / mass for w, (_, scale) in zip(weights, heads)]
     groups = BLOCKS
     rows = by_block([t for w in weights for t in (w, pltpu.roll(w, 4, 0))])
-    at = iota((PAIRS, LANES), 1) % PAIRS == iota((PAIRS, LANES), 0)
-    spread = jnp.concatenate(
-        [jnp.where(at, rows[g : g + 1], 0.0) for g in range(groups)], axis=1
-    )
-    members = [k * groups + g for g in range(groups) for k in range(BLOCKS)]
-    out = split_dot(spread, stack(flat, members))
+    parts = [
+        weighted_sum(flat, rows[g : g + 1], [k * groups + g for k in range(BLOCKS)])
+        for g in range(groups)
+    ]
+    out = (parts[0] + parts[1]) + (parts[2] + parts[3])
     power = power_of(out)
     payload = fixed(jnp.concatenate([coded(out, power), header(lse, power)], axis=0))
     sent = out_ref.reshape(out_ref.shape[0], PAY, HD)
@@ -218,27 +210,25 @@
     mass = functools.reduce(jnp.add, weights)
     lse = peak + jnp.log(mass)
     weights = by_block([w * scale / mass for w, (_, scale) in zip(weights, heads)])
-    pair = iota((PAIRS, LANES), 0)
-    at = lax.rem(iota((PAIRS, LANES), 1), PAIRS) == lax.rem(pair, ROWS) * HALF + pair // ROWS
     heads = []
     for g in range(groups):
-        out = split_dot(jnp.where(at, weights[g : g + 1], 0.0), stack(flat, [groups * y + g for y in range(BLOCKS)]))
+        out = weighted_sum(
+            flat, weights[g : g + 1], [groups * y + g for y in range(BLOCKS)]
+        )
         heads.extend(out[ROWS * h : ROWS * (h + 1)] for h in range(HALF))
     attended = jnp.concatenate(heads, axis=1).astype(jnp.bfloat16)
     proj_ref[...] = lax.dot_general(
         attended, w_ref[...], (((1,), (1,)), ((), ())), preferred_element_type=jnp.float32
     )
-    sub, lane = iota((8, LANES), 0), iota((8, LANES), 1)
-    result = jnp.zeros((8, LANES), jnp.float32)
+    pair, lane = iota((PAIRS, LANES), 0), iota((PAIRS, LANES), 1)
+    table = jnp.zeros((PAIRS, LANES), jnp.float32)
     for c in range(2):
-        own = jnp.sum(
-            jnp.where(sub == lax.axis_index("x") * 2 + c, lse, 0.0), axis=0, keepdims=True
-        )
-        own = jnp.broadcast_to(own, (8, LANES))
-        for r in range(ROWS):
-            shifted = pltpu.roll(own, (LANES + c * HALF - r * HALF) % LANES, 1)
-            result = jnp.where((sub == r) & (lane // HALF == c), shifted, result)
-    mass_ref[...] = result[:ROWS, :GROUP]
+        mine = iota(lse.shape, 0) == lax.axis_index("x") * 2 + c
+        own = jnp.sum(jnp.where(mine, lse, 0.0), axis=0, keepdims=True)
+        column = jnp.sum(jnp.where(lane == pair, own, 0.0), axis=1, keepdims=True)
+        table = jnp.where(lane == c * HALF + pair // ROWS, column, table)
+    table = sum(table[8 * i : 8 * (i + 1)] for i in range(PAIRS // 8))
+    mass_ref[...] = (table[:ROWS] + table[ROWS:])[:, :GROUP]
 
 
 def shards(queries, keys, values, lengths, span_map, w_out):
@@ -263,6 +253,7 @@
             pltpu.VMEM((ROWS, GROUP, LANES), f32),
             pltpu.VMEM((ROWS, GROUP, LANES), f32),
             pltpu.VMEM((ROWS, GROUP, HD), f32),
+            pltpu.VMEM((2, 3, PAIRS, LANES), f32),
             pltpu.SemaphoreType.DMA((3,)),
             pltpu.SemaphoreType.DMA((len(KEY_PARTS),)),
             pltpu.SemaphoreType.DMA((len(VALUE_PARTS),)),

time: 42.3 us -> 42.1 us (level)
  no operation moved by 1% of the time
where the time goes in v5:
time: 42.1 us; the launch traced here: 42 us
  blocking collectives  35.2 us (84%)
  Pallas kernels  6.14 us (15%)
  between operations  0.66 us (2%)
    all_to_all x1, blocking collectives, shards(): part = lax.all_to_all(part, ('z', 'core'), 0, 0, tiled=True)  19.1 us
    all_to_all x1, blocking collectives, shards(): part = lax.all_to_all(part, ('y', 'x', 'core'), 0, 0, tiled=True)  16.1 us
    pallas_call x1, Pallas kernels, shards(): pl.pallas_call(attend_kernel, out_shape=pltpu.VMEM((z * 2, PAY // 2, 2, H...  4.27 us
    pallas_call x1, Pallas kernels, shards(): pl.pallas_call(project_kernel, out_shape=(jax.ShapeDtypeStruct((ROWS, w_o...  1.29 us

profile of v5, /device:TPU:1, one launch (start us, length us, event | category | flops | bytes accessed | tf_op | source)
XLA Modules:
  0.0 42.0 jit_solution(5077851487409974680)
XLA Ops:
  0.6 0.0 copy-start
  0.6 4.3 %attend.1 = s16[16,17,2,128]{3,2,1,0:T(2,128)(2,1)S(1)} custom-call(bf16[4,16,128]{2,1,0:T(8,128)(2,1)} %q_hbm.1, s32[4]{0:T(128)} %len_hbm.1, s32[32]{0:T(128)} %map_hbm.1, bf16[32,512,128]{2,1,0:T(8,128)(2,1)} %bitcast.4, bf16[32,512,128]{2,1,0:T(8,128)(2,1)} %bitcast.5), custom_call_target="tpu_custom_call" | custom-call | tf_op jit(solution)/shard_map/attend/pallas_call | solution.py:241
  4.9 19.1 %all_to_all.10.in_ref = s16[16,17,2,128]{3,2,1,0:T(2,128)(2,1)S(1)} all-to-all(s16[16,17,2,128]{3,2,1,0:T(2,128)(2,1)S(1)} %attend.1), channel_id=1, replica_groups=mesh['z'=8,'y'=4,'core'=2,'x'=4] {'z','core'}, dimensions={0} | all-to-all | bytes 278528 | tf_op jit(solution)/shard_map/all_to_all | solution.py:264
  24.0 0.6 %merge.1 = s16[32,17,2,128]{3,2,1,0:T(2,128)(2,1)S(1)} custom-call(s16[16,17,2,128]{3,2,1,0:T(2,128)(2,1)S(1)} %all_to_all.10.in_ref), custom_call_target="tpu_custom_call" | custom-call | tf_op jit(solution)/shard_map/merge/pallas_call | solution.py:265
  24.6 16.1 %all_to_all.11.in_ref = s16[32,17,2,128]{3,2,1,0:T(2,128)(2,1)S(1)} all-to-all(s16[32,17,2,128]{3,2,1,0:T(2,128)(2,1)S(1)} %merge.1), channel_id=1, replica_groups=mesh['z'=8,'y'=4,'core'=2,'x'=4] {'y','x','core'}, dimensions={0} | all-to-all | bytes 557056 | tf_op jit(solution)/shard_map/all_to_all | solution.py:273
  40.7 0.0 copy-done
  40.7 1.3 %project.1 = (f32[4,64]{1,0:T(4,128)}, f32[4,16]{1,0:T(4,128)}) custom-call(s16[32,17,2,128]{3,2,1,0:T(2,128)(2,1)S(1)} %all_to_all.11.in_ref, bf16[64,8192]{1,0:T(8,128)(2,1)S(1)} %bitcast.3), custom_call_target="tpu_custom_call" | custom-call | tf_op jit(solution)/shard_map/project/pallas_call | solution.py:274
Async XLA Ops:
  0.6 40.1 %copy-start = (bf16[8192,64]{0,1:T(8,128)(2,1)S(1)}, bf16[8192,64]{0,1:T(8,128)(2,1)}, u32[]{:S(2)}) copy-start(bf16[8192,64]{0,1:T(8,128)(2,1)} %param.11) | copy-start | bytes 3145732

commit v6 on v5

--- a/solution.py
+++ b/solution.py
@@ -38,8 +38,8 @@
 def header(lse, power):
     whole = jnp.floor(lse)
     rest = (lse - whole) * 32768.0
-    first = jnp.floor(rest)
-    second = jnp.floor((rest - first) * 32768.0)
+    first = jnp.minimum(jnp.floor(rest), 32767.0)
+    second = jnp.minimum(jnp.floor((rest - first) * 32768.0), 32767.0)
     shape = (PAIRS, LANES)
     block = iota(shape, 1) // PAIRS
     kind = jnp.where(block == 0, whole, jnp.where(block == 1, first, second))

time: 42.1 us -> 42.1 us (level)
  no operation moved by 1% of the time
where the time goes in v6:
time: 42.1 us; the launch traced here: 42 us
  blocking collectives  35.2 us (84%)
  Pallas kernels  6.14 us (15%)
  between operations  0.66 us (2%)
    all_to_all x1, blocking collectives, shards(): part = lax.all_to_all(part, ('z', 'core'), 0, 0, tiled=True)  19.1 us
    all_to_all x1, blocking collectives, shards(): part = lax.all_to_all(part, ('y', 'x', 'core'), 0, 0, tiled=True)  16.1 us
    pallas_call x1, Pallas kernels, shards(): pl.pallas_call(attend_kernel, out_shape=pltpu.VMEM((z * 2, PAY // 2, 2, H...  4.27 us
    pallas_call x1, Pallas kernels, shards(): pl.pallas_call(project_kernel, out_shape=(jax.ShapeDtypeStruct((ROWS, w_o...  1.29 us

profile of v6, /device:TPU:1, one launch (start us, length us, event | category | flops | bytes accessed | tf_op | source)
XLA Modules:
  0.0 42.0 jit_solution(3873843242933248988)
XLA Ops:
  0.6 0.0 copy-start
  0.6 4.3 %attend.1 = s16[16,17,2,128]{3,2,1,0:T(2,128)(2,1)S(1)} custom-call(bf16[4,16,128]{2,1,0:T(8,128)(2,1)} %q_hbm.1, s32[4]{0:T(128)} %len_hbm.1, s32[32]{0:T(128)} %map_hbm.1, bf16[32,512,128]{2,1,0:T(8,128)(2,1)} %bitcast.4, bf16[32,512,128]{2,1,0:T(8,128)(2,1)} %bitcast.5), custom_call_target="tpu_custom_call" | custom-call | tf_op jit(solution)/shard_map/attend/pallas_call | solution.py:241
  4.9 19.1 %all_to_all.10.in_ref = s16[16,17,2,128]{3,2,1,0:T(2,128)(2,1)S(1)} all-to-all(s16[16,17,2,128]{3,2,1,0:T(2,128)(2,1)S(1)} %attend.1), channel_id=1, replica_groups=mesh['z'=8,'y'=4,'core'=2,'x'=4] {'z','core'}, dimensions={0} | all-to-all | bytes 278528 | tf_op jit(solution)/shard_map/all_to_all | solution.py:264
  24.0 0.6 %merge.1 = s16[32,17,2,128]{3,2,1,0:T(2,128)(2,1)S(1)} custom-call(s16[16,17,2,128]{3,2,1,0:T(2,128)(2,1)S(1)} %all_to_all.10.in_ref), custom_call_target="tpu_custom_call" | custom-call | tf_op jit(solution)/shard_map/merge/pallas_call | solution.py:265
  24.6 16.1 %all_to_all.11.in_ref = s16[32,17,2,128]{3,2,1,0:T(2,128)(2,1)S(1)} all-to-all(s16[32,17,2,128]{3,2,1,0:T(2,128)(2,1)S(1)} %merge.1), channel_id=1, replica_groups=mesh['z'=8,'y'=4,'core'=2,'x'=4] {'y','x','core'}, dimensions={0} | all-to-all | bytes 557056 | tf_op jit(solution)/shard_map/all_to_all | solution.py:273
  40.7 0.0 copy-done
  40.7 1.3 %project.1 = (f32[4,64]{1,0:T(4,128)}, f32[4,16]{1,0:T(4,128)}) custom-call(s16[32,17,2,128]{3,2,1,0:T(2,128)(2,1)S(1)} %all_to_all.11.in_ref, bf16[64,8192]{1,0:T(8,128)(2,1)S(1)} %bitcast.3), custom_call_target="tpu_custom_call" | custom-call | tf_op jit(solution)/shard_map/project/pallas_call | solution.py:274
Async XLA Ops:
  0.6 40.0 %copy-start = (bf16[8192,64]{0,1:T(8,128)(2,1)S(1)}, bf16[8192,64]{0,1:T(8,128)(2,1)}, u32[]{:S(2)}) copy-start(bf16[8192,64]{0,1:T(8,128)(2,1)} %param.11) | copy-start | bytes 3145732

commit v7 on v6

--- a/solution.py
+++ b/solution.py
@@ -201,21 +201,35 @@
         sent[i] = payload
 
 
-def project_kernel(in_ref, w_ref, proj_ref, mass_ref):
+def gather_kernel(in_ref, out_ref):
     flat = in_ref.reshape(in_ref.shape[0], PAY, HD)
     groups = in_ref.shape[0] // BLOCKS
-    heads = [read_headers(flat, range(groups * y, groups * (y + 1))) for y in range(BLOCKS)]
-    peak = functools.reduce(jnp.maximum, [lse for lse, _ in heads])
+    heads = [read_headers(flat, range(8 * t, 8 * t + 8)) for t in range(2)]
+    peak = jnp.maximum(heads[0][0], heads[1][0])
+    peak = jnp.maximum(peak, pltpu.roll(peak, 4, 0))
     weights = [jnp.exp(lse - peak) for lse, _ in heads]
-    mass = functools.reduce(jnp.add, weights)
-    lse = peak + jnp.log(mass)
-    weights = by_block([w * scale / mass for w, (_, scale) in zip(weights, heads)])
-    heads = []
+    mass = weights[0] + weights[1]
+    mass = mass + pltpu.roll(mass, 4, 0)
+    weights = [w * scale / mass for w, (_, scale) in zip(weights, heads)]
+    rows = by_block([t for w in weights for t in (w, pltpu.roll(w, 4, 0))])
     for g in range(groups):
-        out = weighted_sum(
-            flat, weights[g : g + 1], [groups * y + g for y in range(BLOCKS)]
+        out_ref[g * PAIRS : (g + 1) * PAIRS] = weighted_sum(
+            flat, rows[g : g + 1], [groups * k + g for k in range(BLOCKS)]
         )
-        heads.extend(out[ROWS * h : ROWS * (h + 1)] for h in range(HALF))
+    out_ref[groups * PAIRS : groups * PAIRS + 8] = peak + jnp.log(mass)
+
+
+def project_kernel(mine_ref, other_ref, w_ref, proj_ref, mass_ref):
+    groups = mine_ref.shape[0] // PAIRS
+    first = lax.axis_index("core") == 0
+    mine, other = mine_ref[...], other_ref[...]
+    halves = [jnp.where(first, mine, other), jnp.where(first, other, mine)]
+    heads = [
+        halves[c][x * PAIRS + ROWS * h : x * PAIRS + ROWS * (h + 1)]
+        for x in range(groups)
+        for c in range(2)
+        for h in range(HALF)
+    ]
     attended = jnp.concatenate(heads, axis=1).astype(jnp.bfloat16)
     proj_ref[...] = lax.dot_general(
         attended, w_ref[...], (((1,), (1,)), ((), ())), preferred_element_type=jnp.float32
@@ -223,8 +237,9 @@
     pair, lane = iota((PAIRS, LANES), 0), iota((PAIRS, LANES), 1)
     table = jnp.zeros((PAIRS, LANES), jnp.float32)
     for c in range(2):
-        mine = iota(lse.shape, 0) == lax.axis_index("x") * 2 + c
-        own = jnp.sum(jnp.where(mine, lse, 0.0), axis=0, keepdims=True)
+        lse = halves[c][groups * PAIRS : groups * PAIRS + 8]
+        own = jnp.where(iota(lse.shape, 0) == lax.axis_index("x"), lse, 0.0)
+        own = jnp.sum(own, axis=0, keepdims=True)
         column = jnp.sum(jnp.where(lane == pair, own, 0.0), axis=1, keepdims=True)
         table = jnp.where(lane == c * HALF + pair // ROWS, column, table)
     table = sum(table[8 * i : 8 * (i + 1)] for i in range(PAIRS // 8))
@@ -264,24 +279,33 @@
     part = lax.all_to_all(part, ("z", "core"), 0, 0, tiled=True)
     part = pl.pallas_call(
         merge_kernel,
-        out_shape=jax.ShapeDtypeStruct((y * x * 2, PAY // 2, 2, HD), jnp.int16),
+        out_shape=jax.ShapeDtypeStruct((y * x, PAY // 2, 2, HD), jnp.int16),
         in_specs=[VMEM],
         out_specs=VMEM,
         compiler_params=pltpu.CompilerParams(vmem_limit_bytes=8 * 2**20),
         name="merge",
     )(part)
-    part = lax.all_to_all(part, ("y", "x", "core"), 0, 0, tiled=True)
+    part = lax.all_to_all(part, ("y", "x"), 0, 0, tiled=True)
+    mine = pl.pallas_call(
+        gather_kernel,
+        out_shape=pltpu.VMEM((x * PAIRS + 8, HD), f32),
+        in_specs=[VMEM],
+        out_specs=VMEM,
+        compiler_params=pltpu.CompilerParams(vmem_limit_bytes=8 * 2**20),
+        name="gather",
+    )(part)
+    other = lax.ppermute(mine, "core", [(0, 1), (1, 0)])
     return pl.pallas_call(
         project_kernel,
         out_shape=(
             jax.ShapeDtypeStruct((ROWS, w_out.shape[1]), f32),
             jax.ShapeDtypeStruct((ROWS, GROUP), f32),
         ),
-        in_specs=[VMEM, VMEM],
+        in_specs=[VMEM, VMEM, VMEM],
         out_specs=(VMEM, VMEM),
         compiler_params=pltpu.CompilerParams(vmem_limit_bytes=8 * 2**20),
         name="project",
-    )(part, w_out.T)
+    )(mine, other, w_out.T)
 
 
 def solution(mesh):

time: 42.1 us -> 41.9 us (level)
  blocking collectives: 35.2 us -> 33.2 us
  waiting for transfers between devices: 0 us -> 0.91 us
  starting transfers between devices: 0 us -> 0.87 us
    all_to_all x1, blocking collectives: 16.1 us -> 14.1 us  [shards(): part = lax.all_to_all(part, ('y', 'x'), 0, 0, tiled=True)]
    ppermute x0 -> x1, waiting for transfers between devices: none -> 0.91 us  [shards(): other = lax.ppermute(mine, 'core', [(0, 1), (1, 0)])]
    ppermute x0 -> x1, starting transfers between devices: none -> 0.87 us  [shards(): other = lax.ppermute(mine, 'core', [(0, 1), (1, 0)])]
  transfers between devices with their start and end apart: 0 -> 1, of which waited for: 0 -> 1; matrix products, arithmetic and copies ran while one was open for 0% -> 0% of each run, Pallas kernels for 0% -> 0%
where the time goes in v7:
time: 41.9 us; the launch traced here: 41.7 us
  blocking collectives  33.2 us (79%)
  Pallas kernels  6.06 us (14%)
  waiting for transfers between devices  0.91 us (2%)
  starting transfers between devices  0.87 us (2%)
  between operations  0.66 us (2%)
    all_to_all x1, blocking collectives, shards(): part = lax.all_to_all(part, ('z', 'core'), 0, 0, tiled=True)  19.1 us
    all_to_all x1, blocking collectives, shards(): part = lax.all_to_all(part, ('y', 'x'), 0, 0, tiled=True)  14.1 us
    pallas_call x1, Pallas kernels, shards(): pl.pallas_call(attend_kernel, out_shape=pltpu.VMEM((z * 2, PAY // 2, 2, H...  4.26 us
    pallas_call x1, Pallas kernels, shards(): pl.pallas_call(project_kernel, out_shape=(jax.ShapeDtypeStruct((ROWS, w_o...  0.97 us
    ppermute x1, waiting for transfers between devices, shards(): other = lax.ppermute(mine, 'core', [(0, 1), (1, 0)])  0.91 us
    ppermute x1, starting transfers between devices, shards(): other = lax.ppermute(mine, 'core', [(0, 1), (1, 0)])  0.87 us
  transfers between devices with their start and end apart: 1, of which 1 were waited for; matrix products, arithmetic and copies ran while one was open for 0% of the time, Pallas kernels for 0%

profile of v7, /device:TPU:1, one launch (start us, length us, event | category | flops | bytes accessed | tf_op | source)
XLA Modules:
  0.0 41.7 jit_solution(11404156214493234818)
XLA Ops:
  0.6 0.0 copy-start
  0.6 4.3 %attend.1 = s16[16,17,2,128]{3,2,1,0:T(2,128)(2,1)S(1)} custom-call(bf16[4,16,128]{2,1,0:T(8,128)(2,1)} %q_hbm.1, s32[4]{0:T(128)} %len_hbm.1, s32[32]{0:T(128)} %map_hbm.1, bf16[32,512,128]{2,1,0:T(8,128)(2,1)} %bitcast.4, bf16[32,512,128]{2,1,0:T(8,128)(2,1)} %bitcast.5), custom_call_target="tpu_custom_call" | custom-call | tf_op jit(solution)/shard_map/attend/pallas_call | solution.py:256
  4.9 19.1 %all_to_all.10.in_ref = s16[16,17,2,128]{3,2,1,0:T(2,128)(2,1)S(1)} all-to-all(s16[16,17,2,128]{3,2,1,0:T(2,128)(2,1)S(1)} %attend.1), channel_id=1, replica_groups=mesh['z'=8,'y'=4,'core'=2,'x'=4] {'z','core'}, dimensions={0} | all-to-all | bytes 278528 | tf_op jit(solution)/shard_map/all_to_all | solution.py:279
  24.0 0.5 %merge.1 = s16[16,17,2,128]{3,2,1,0:T(2,128)(2,1)S(1)} custom-call(s16[16,17,2,128]{3,2,1,0:T(2,128)(2,1)S(1)} %all_to_all.10.in_ref), custom_call_target="tpu_custom_call" | custom-call | tf_op jit(solution)/shard_map/merge/pallas_call | solution.py:280
  24.5 14.1 %all_to_all.11.in_ref = s16[16,17,2,128]{3,2,1,0:T(2,128)(2,1)S(1)} all-to-all(s16[16,17,2,128]{3,2,1,0:T(2,128)(2,1)S(1)} %merge.1), channel_id=1, replica_groups=mesh['z'=8,'y'=4,'core'=2,'x'=4] {'y','x'}, dimensions={0} | all-to-all | bytes 278528 | tf_op jit(solution)/shard_map/all_to_all | solution.py:288
  38.6 0.3 gather.1.mine_ref
  39.0 0.9 %collective-permute-start = (f32[136,128]{1,0:T(8,128)S(1)}, f32[136,128]{1,0:T(8,128)S(1)}, u32[]{:S(2)}, u32[]{:S(2)}) collective-permute-start(f32[136,128]{1,0:T(8,128)S(1)} %gather.1.mine_ref), channel_id=1, source_target_pairs={{0,4},{4,0},{1,5},{5,1},{2,6},{6,2},{3,7},{7,3},{8,12},{12,8},{9,1... | collective-permute-start | bytes 208904 | tf_op jit(solution)/shard_map/ppermute | solution.py:297
  39.8 0.9 %collective-permute-done.other_ref = f32[136,128]{1,0:T(8,128)S(1)} collective-permute-done((f32[136,128]{1,0:T(8,128)S(1)}, f32[136,128]{1,0:T(8,128)S(1)}, u32[]{:S(2)}, u32[]{:S(2)}) %collective-permute-start) | collective-permute-done | bytes 69664 | tf_op jit(solution)/shard_map/ppermute | solution.py:297
  40.7 0.0 copy-done
  40.7 1.0 %project.1 = (f32[4,64]{1,0:T(4,128)}, f32[4,16]{1,0:T(4,128)}) custom-call(f32[136,128]{1,0:T(8,128)S(1)} %gather.1.mine_ref, f32[136,128]{1,0:T(8,128)S(1)} %collective-permute-done.other_ref, bf16[64,8192]{1,0:T(8,128)(2,1)S(1)} %bitcast.3), custom_call_target="tpu_custom_call" | custom-call | tf_op jit(solution)/shard_map/project/pallas_call | solution.py:298
Async XLA Ops:
  0.6 40.1 %copy-start = (bf16[8192,64]{0,1:T(8,128)(2,1)S(1)}, bf16[8192,64]{0,1:T(8,128)(2,1)}, u32[]{:S(2)}) copy-start(bf16[8192,64]{0,1:T(8,128)(2,1)} %param.11) | copy-start | bytes 3145732
  39.0 1.8 %collective-permute-start = (f32[136,128]{1,0:T(8,128)S(1)}, f32[136,128]{1,0:T(8,128)S(1)}, u32[]{:S(2)}, u32[]{:S(2)}) collective-permute-start(f32[136,128]{1,0:T(8,128)S(1)} %gather.1.mine_ref), channel_id=1, source_target_pairs={{0,4},{4,0},{1,5},{5,1},{2,6},{6,2},{3,7},{7,3},{8,12},{12,8},{9,1... | collective-permute-start | bytes 208904 | tf_op jit(solution)/shard_map/ppermute | solution.py:297

commit v8 on v7

--- a/solution.py
+++ b/solution.py
@@ -219,25 +219,41 @@
     out_ref[groups * PAIRS : groups * PAIRS + 8] = peak + jnp.log(mass)
 
 
-def project_kernel(mine_ref, other_ref, w_ref, proj_ref, mass_ref):
-    groups = mine_ref.shape[0] // PAIRS
-    first = lax.axis_index("core") == 0
-    mine, other = mine_ref[...], other_ref[...]
-    halves = [jnp.where(first, mine, other), jnp.where(first, other, mine)]
+def half_product(ref, w_ref, c):
+    groups = ref.shape[0] // PAIRS
+    half = ref[...]
+    wide = HALF * HD
     heads = [
-        halves[c][x * PAIRS + ROWS * h : x * PAIRS + ROWS * (h + 1)]
+        half[x * PAIRS + ROWS * h : x * PAIRS + ROWS * (h + 1)]
         for x in range(groups)
-        for c in range(2)
         for h in range(HALF)
     ]
-    attended = jnp.concatenate(heads, axis=1).astype(jnp.bfloat16)
-    proj_ref[...] = lax.dot_general(
-        attended, w_ref[...], (((1,), (1,)), ((), ())), preferred_element_type=jnp.float32
+    columns = [
+        w_ref[:, pl.ds(pl.multiple_of((x * 2 + c) * wide, wide), wide)] for x in range(groups)
+    ]
+    return lax.dot_general(
+        jnp.concatenate(heads, axis=1).astype(jnp.bfloat16),
+        jnp.concatenate(columns, axis=1),
+        (((1,), (1,)), ((), ())),
+        preferred_element_type=jnp.float32,
     )
+
+
+def own_kernel(mine_ref, w_ref, out_ref):
+    out_ref[...] = half_product(mine_ref, w_ref, lax.axis_index("core"))
+
+
+def project_kernel(mine_ref, other_ref, own_ref, w_ref, proj_ref, mass_ref):
+    groups = mine_ref.shape[0] // PAIRS
+    core = lax.axis_index("core")
+    proj_ref[...] = own_ref[...] + half_product(other_ref, w_ref, 1 - core)
+    tail = slice(groups * PAIRS, groups * PAIRS + 8)
+    mine, other = mine_ref[tail], other_ref[tail]
+    halves = [jnp.where(core == 0, mine, other), jnp.where(core == 0, other, mine)]
     pair, lane = iota((PAIRS, LANES), 0), iota((PAIRS, LANES), 1)
     table = jnp.zeros((PAIRS, LANES), jnp.float32)
     for c in range(2):
-        lse = halves[c][groups * PAIRS : groups * PAIRS + 8]
+        lse = halves[c]
         own = jnp.where(iota(lse.shape, 0) == lax.axis_index("x"), lse, 0.0)
         own = jnp.sum(own, axis=0, keepdims=True)
         column = jnp.sum(jnp.where(lane == pair, own, 0.0), axis=1, keepdims=True)
@@ -295,17 +311,28 @@
         name="gather",
     )(part)
     other = lax.ppermute(mine, "core", [(0, 1), (1, 0)])
+    own = pl.pallas_call(
+        own_kernel,
+        out_shape=pltpu.VMEM((ROWS, w_out.shape[1]), f32),
+        in_specs=[VMEM, VMEM],
+        out_specs=VMEM,
+        compiler_params=pltpu.CompilerParams(vmem_limit_bytes=8 * 2**20),
+        cost_estimate=pl.CostEstimate(
+            flops=ROWS * w_out.size, bytes_accessed=w_out.size, transcendentals=0
+        ),
+        name="own",
+    )(mine, w_out.T)
     return pl.pallas_call(
         project_kernel,
         out_shape=(
             jax.ShapeDtypeStruct((ROWS, w_out.shape[1]), f32),
             jax.ShapeDtypeStruct((ROWS, GROUP), f32),
         ),
-        in_specs=[VMEM, VMEM, VMEM],
+        in_specs=[VMEM] * 4,
         out_specs=(VMEM, VMEM),
         compiler_params=pltpu.CompilerParams(vmem_limit_bytes=8 * 2**20),
         name="project",
-    )(mine, other, w_out.T)
+    )(mine, other, own, w_out.T)
 
 
 def solution(mesh):

time: 41.9 us -> 41.7 us (level)
  transfers between devices with their start and end apart: 1 -> 1, of which waited for: 1 -> 1; matrix products, arithmetic and copies ran while one was open for 0% -> 0% of each run, Pallas kernels for 0% -> 1%
where the time goes in v8:
time: 41.7 us; the launch traced here: 41.6 us
  blocking collectives  33.2 us (80%)
  Pallas kernels  6.17 us (15%)
  starting transfers between devices  0.87 us (2%)
  between operations  0.67 us (2%)
  waiting for transfers between devices  0.66 us (2%)
    all_to_all x1, blocking collectives, shards(): part = lax.all_to_all(part, ('z', 'core'), 0, 0, tiled=True)  19.1 us
    all_to_all x1, blocking collectives, shards(): part = lax.all_to_all(part, ('y', 'x'), 0, 0, tiled=True)  14.1 us
    pallas_call x1, Pallas kernels, shards(): pl.pallas_call(attend_kernel, out_shape=pltpu.VMEM((z * 2, PAY // 2, 2, H...  4.27 us
    ppermute x1, starting transfers between devices, shards(): other = lax.ppermute(mine, 'core', [(0, 1), (1, 0)])  0.87 us
    pallas_call x1, Pallas kernels, shards(): pl.pallas_call(project_kernel, out_shape=(jax.ShapeDtypeStruct((ROWS, w_o...  0.84 us
  transfers between devices with their start and end apart: 1, of which 1 were waited for; matrix products, arithmetic and copies ran while one was open for 0% of the time, Pallas kernels for 1%

profile of v8, /device:TPU:1, one launch (start us, length us, event | category | flops | bytes accessed | tf_op | source)
XLA Modules:
  0.0 41.6 jit_solution(13787687430125692877)
XLA Ops:
  0.6 0.0 copy-start
  0.6 4.3 %attend.1 = s16[16,17,2,128]{3,2,1,0:T(2,128)(2,1)S(1)} custom-call(bf16[4,16,128]{2,1,0:T(8,128)(2,1)} %q_hbm.1, s32[4]{0:T(128)} %len_hbm.1, s32[32]{0:T(128)} %map_hbm.1, bf16[32,512,128]{2,1,0:T(8,128)(2,1)} %bitcast.5, bf16[32,512,128]{2,1,0:T(8,128)(2,1)} %bitcast.6), custom_call_target="tpu_custom_call" | custom-call | tf_op jit(solution)/shard_map/attend/pallas_call | solution.py:272
  4.9 19.1 %all_to_all.10.in_ref = s16[16,17,2,128]{3,2,1,0:T(2,128)(2,1)S(1)} all-to-all(s16[16,17,2,128]{3,2,1,0:T(2,128)(2,1)S(1)} %attend.1), channel_id=1, replica_groups=mesh['z'=8,'y'=4,'core'=2,'x'=4] {'z','core'}, dimensions={0} | all-to-all | bytes 278528 | tf_op jit(solution)/shard_map/all_to_all | solution.py:295
  24.0 0.5 %merge.1 = s16[16,17,2,128]{3,2,1,0:T(2,128)(2,1)S(1)} custom-call(s16[16,17,2,128]{3,2,1,0:T(2,128)(2,1)S(1)} %all_to_all.10.in_ref), custom_call_target="tpu_custom_call" | custom-call | tf_op jit(solution)/shard_map/merge/pallas_call | solution.py:296
  24.5 14.1 %all_to_all.11.in_ref = s16[16,17,2,128]{3,2,1,0:T(2,128)(2,1)S(1)} all-to-all(s16[16,17,2,128]{3,2,1,0:T(2,128)(2,1)S(1)} %merge.1), channel_id=1, replica_groups=mesh['z'=8,'y'=4,'core'=2,'x'=4] {'y','x'}, dimensions={0} | all-to-all | bytes 278528 | tf_op jit(solution)/shard_map/all_to_all | solution.py:304
  38.6 0.3 gather.1.mine_ref
  39.0 0.9 %collective-permute-start = (f32[136,128]{1,0:T(8,128)S(1)}, f32[136,128]{1,0:T(8,128)S(1)}, u32[]{:S(2)}, u32[]{:S(2)}) collective-permute-start(f32[136,128]{1,0:T(8,128)S(1)} %gather.1.mine_ref), channel_id=1, source_target_pairs={{0,4},{4,0},{1,5},{5,1},{2,6},{6,2},{3,7},{7,3},{8,12},{12,8},{9,1... | collective-permute-start | bytes 208904 | tf_op jit(solution)/shard_map/ppermute | solution.py:313
  39.8 0.0 copy-done
  39.8 0.2 own.1.own_ref
  40.1 0.7 %collective-permute-done.other_ref = f32[136,128]{1,0:T(8,128)S(1)} collective-permute-done((f32[136,128]{1,0:T(8,128)S(1)}, f32[136,128]{1,0:T(8,128)S(1)}, u32[]{:S(2)}, u32[]{:S(2)}) %collective-permute-start) | collective-permute-done | bytes 69664 | tf_op jit(solution)/shard_map/ppermute | solution.py:313
  40.7 0.8 %project.1 = (f32[4,64]{1,0:T(4,128)}, f32[4,16]{1,0:T(4,128)}) custom-call(f32[136,128]{1,0:T(8,128)S(1)} %gather.1.mine_ref, f32[136,128]{1,0:T(8,128)S(1)} %collective-permute-done.other_ref, f32[4,64]{1,0:T(4,128)S(1)} %own.1.own_ref, bf16[64,8192]{1,0:T(8,128)(2,1)S(1)} %bitcast.4), custom_call_target="tpu_custom_call" | custom-call | tf_op jit(solution)/shard_map/project/pallas_call | solution.py:325
Async XLA Ops:
  0.6 39.2 %copy-start = (bf16[8192,64]{0,1:T(8,128)(2,1)S(1)}, bf16[8192,64]{0,1:T(8,128)(2,1)}, u32[]{:S(2)}) copy-start(bf16[8192,64]{0,1:T(8,128)(2,1)} %param.11) | copy-start | bytes 3145732
  39.0 1.8 %collective-permute-start = (f32[136,128]{1,0:T(8,128)S(1)}, f32[136,128]{1,0:T(8,128)S(1)}, u32[]{:S(2)}, u32[]{:S(2)}) collective-permute-start(f32[136,128]{1,0:T(8,128)S(1)} %gather.1.mine_ref), channel_id=1, source_target_pairs={{0,4},{4,0},{1,5},{5,1},{2,6},{6,2},{3,7},{7,3},{8,12},{12,8},{9,1... | collective-permute-start | bytes 208904 | tf_op jit(solution)/shard_map/ppermute | solution.py:313

commit v9 on v8

--- a/solution.py
+++ b/solution.py
@@ -239,27 +239,27 @@
     )
 
 
-def own_kernel(mine_ref, w_ref, out_ref):
-    out_ref[...] = half_product(mine_ref, w_ref, lax.axis_index("core"))
-
-
-def project_kernel(mine_ref, other_ref, own_ref, w_ref, proj_ref, mass_ref):
-    groups = mine_ref.shape[0] // PAIRS
+def mass_rows(ref, c):
+    tile = ref[ref.shape[0] - 8 : ref.shape[0]]
+    own = jnp.where(iota(tile.shape, 0) == lax.axis_index("x"), tile, 0.0)
+    own = jnp.sum(own, axis=0, keepdims=True)
+    pair, lane = iota((PAIRS, LANES), 0), iota((PAIRS, LANES), 1)
+    column = jnp.sum(jnp.where(lane == pair, own, 0.0), axis=1, keepdims=True)
+    table = jnp.where(lane == c * HALF + pair // ROWS, column, 0.0)
+    table = sum(table[8 * i : 8 * (i + 1)] for i in range(PAIRS // 8))
+    return (table[:ROWS] + table[ROWS:])[:, :GROUP]
+
+
+def own_kernel(mine_ref, w_ref, out_ref, mass_ref):
     core = lax.axis_index("core")
-    proj_ref[...] = own_ref[...] + half_product(other_ref, w_ref, 1 - core)
-    tail = slice(groups * PAIRS, groups * PAIRS + 8)
-    mine, other = mine_ref[tail], other_ref[tail]
-    halves = [jnp.where(core == 0, mine, other), jnp.where(core == 0, other, mine)]
-    pair, lane = iota((PAIRS, LANES), 0), iota((PAIRS, LANES), 1)
-    table = jnp.zeros((PAIRS, LANES), jnp.float32)
-    for c in range(2):
-        lse = halves[c]
-        own = jnp.where(iota(lse.shape, 0) == lax.axis_index("x"), lse, 0.0)
-        own = jnp.sum(own, axis=0, keepdims=True)
-        column = jnp.sum(jnp.where(lane == pair, own, 0.0), axis=1, keepdims=True)
-        table = jnp.where(lane == c * HALF + pair // ROWS, column, table)
-    table = sum(table[8 * i : 8 * (i + 1)] for i in range(PAIRS // 8))
-    mass_ref[...] = (table[:ROWS] + table[ROWS:])[:, :GROUP]
+    out_ref[...] = half_product(mine_ref, w_ref, core)
+    mass_ref[...] = mass_rows(mine_ref, core)
+
+
+def project_kernel(other_ref, own_ref, own_mass_ref, w_ref, proj_ref, mass_ref):
+    other = 1 - lax.axis_index("core")
+    proj_ref[...] = own_ref[...] + half_product(other_ref, w_ref, other)
+    mass_ref[...] = own_mass_ref[...] + mass_rows(other_ref, other)
 
 
 def shards(queries, keys, values, lengths, span_map, w_out):
@@ -311,11 +311,14 @@
         name="gather",
     )(part)
     other = lax.ppermute(mine, "core", [(0, 1), (1, 0)])
-    own = pl.pallas_call(
+    own, own_mass = pl.pallas_call(
         own_kernel,
-        out_shape=pltpu.VMEM((ROWS, w_out.shape[1]), f32),
+        out_shape=(
+            pltpu.VMEM((ROWS, w_out.shape[1]), f32),
+            pltpu.VMEM((ROWS, GROUP), f32),
+        ),
         in_specs=[VMEM, VMEM],
-        out_specs=VMEM,
+        out_specs=(VMEM, VMEM),
         compiler_params=pltpu.CompilerParams(vmem_limit_bytes=8 * 2**20),
         cost_estimate=pl.CostEstimate(
             flops=ROWS * w_out.size, bytes_accessed=w_out.size, transcendentals=0
@@ -332,7 +335,7 @@
         out_specs=(VMEM, VMEM),
         compiler_params=pltpu.CompilerParams(vmem_limit_bytes=8 * 2**20),
         name="project",
-    )(mine, other, own, w_out.T)
+    )(other, own, own_mass, w_out.T)
 
 
 def solution(mesh):

time: 41.7 us -> 41.7 us (level)
  no operation moved by 1% of the time
where the time goes in v9:
time: 41.7 us; the launch traced here: 41.6 us
  blocking collectives  33.2 us (80%)
  Pallas kernels  6.17 us (15%)
  starting transfers between devices  0.87 us (2%)
  between operations  0.67 us (2%)
  waiting for transfers between devices  0.66 us (2%)
    all_to_all x1, blocking collectives, shards(): part = lax.all_to_all(part, ('z', 'core'), 0, 0, tiled=True)  19.1 us
    all_to_all x1, blocking collectives, shards(): part = lax.all_to_all(part, ('y', 'x'), 0, 0, tiled=True)  14.1 us
    pallas_call x1, Pallas kernels, shards(): pl.pallas_call(attend_kernel, out_shape=pltpu.VMEM((z * 2, PAY // 2, 2, H...  4.26 us
    ppermute x1, starting transfers between devices, shards(): other = lax.ppermute(mine, 'core', [(0, 1), (1, 0)])  0.87 us
    pallas_call x1, Pallas kernels, shards(): pl.pallas_call(project_kernel, out_shape=(jax.ShapeDtypeStruct((ROWS, w_o...  0.84 us
  transfers between devices with their start and end apart: 1, of which 1 were waited for; matrix products, arithmetic and copies ran while one was open for 0% of the time, Pallas kernels for 1%

profile of v9, /device:TPU:1, one launch (start us, length us, event | category | flops | bytes accessed | tf_op | source)
XLA Modules:
  0.0 41.6 jit_solution(6574244313702408454)
XLA Ops:
  0.6 0.0 copy-start
  0.6 4.3 %attend.1 = s16[16,17,2,128]{3,2,1,0:T(2,128)(2,1)S(1)} custom-call(bf16[4,16,128]{2,1,0:T(8,128)(2,1)} %q_hbm.1, s32[4]{0:T(128)} %len_hbm.1, s32[32]{0:T(128)} %map_hbm.1, bf16[32,512,128]{2,1,0:T(8,128)(2,1)} %bitcast.5, bf16[32,512,128]{2,1,0:T(8,128)(2,1)} %bitcast.6), custom_call_target="tpu_custom_call" | custom-call | tf_op jit(solution)/shard_map/attend/pallas_call | solution.py:272
  4.9 19.1 %all_to_all.10.in_ref = s16[16,17,2,128]{3,2,1,0:T(2,128)(2,1)S(1)} all-to-all(s16[16,17,2,128]{3,2,1,0:T(2,128)(2,1)S(1)} %attend.1), channel_id=1, replica_groups=mesh['z'=8,'y'=4,'core'=2,'x'=4] {'z','core'}, dimensions={0} | all-to-all | bytes 278528 | tf_op jit(solution)/shard_map/all_to_all | solution.py:295
  24.0 0.5 %merge.1 = s16[16,17,2,128]{3,2,1,0:T(2,128)(2,1)S(1)} custom-call(s16[16,17,2,128]{3,2,1,0:T(2,128)(2,1)S(1)} %all_to_all.10.in_ref), custom_call_target="tpu_custom_call" | custom-call | tf_op jit(solution)/shard_map/merge/pallas_call | solution.py:296
  24.5 14.1 %all_to_all.11.in_ref = s16[16,17,2,128]{3,2,1,0:T(2,128)(2,1)S(1)} all-to-all(s16[16,17,2,128]{3,2,1,0:T(2,128)(2,1)S(1)} %merge.1), channel_id=1, replica_groups=mesh['z'=8,'y'=4,'core'=2,'x'=4] {'y','x'}, dimensions={0} | all-to-all | bytes 278528 | tf_op jit(solution)/shard_map/all_to_all | solution.py:304
  38.6 0.3 gather.1.mine_ref
  39.0 0.9 %collective-permute-start = (f32[136,128]{1,0:T(8,128)S(1)}, f32[136,128]{1,0:T(8,128)S(1)}, u32[]{:S(2)}, u32[]{:S(2)}) collective-permute-start(f32[136,128]{1,0:T(8,128)S(1)} %gather.1.mine_ref), channel_id=1, source_target_pairs={{0,4},{4,0},{1,5},{5,1},{2,6},{6,2},{3,7},{7,3},{8,12},{12,8},{9,1... | collective-permute-start | bytes 208904 | tf_op jit(solution)/shard_map/ppermute | solution.py:313
  39.8 0.0 copy-done
  39.8 0.2 own.1
  40.1 0.7 %collective-permute-done.other_ref = f32[136,128]{1,0:T(8,128)S(1)} collective-permute-done((f32[136,128]{1,0:T(8,128)S(1)}, f32[136,128]{1,0:T(8,128)S(1)}, u32[]{:S(2)}, u32[]{:S(2)}) %collective-permute-start) | collective-permute-done | bytes 69664 | tf_op jit(solution)/shard_map/ppermute | solution.py:313
  40.7 0.8 %project.1 = (f32[4,64]{1,0:T(4,128)}, f32[4,16]{1,0:T(4,128)}) custom-call(f32[136,128]{1,0:T(8,128)S(1)} %collective-permute-done.other_ref, f32[4,64]{1,0:T(4,128)S(1)} %get-tuple-element.4.own_ref, f32[4,16]{1,0:T(4,128)S(1)} %get-tuple-element.5.own_mass_ref, bf16[64,8192]{1,0:T(8,128)(2,1)S(1)} %bitcast.4), custom_call_target="tpu_custom_call" | custom-call | tf_op jit(solution)/shard_map/project/pallas_call | solution.py:328
Async XLA Ops:
  0.6 39.2 %copy-start = (bf16[8192,64]{0,1:T(8,128)(2,1)S(1)}, bf16[8192,64]{0,1:T(8,128)(2,1)}, u32[]{:S(2)}) copy-start(bf16[8192,64]{0,1:T(8,128)(2,1)} %param.11) | copy-start | bytes 3145732
  39.0 1.8 %collective-permute-start = (f32[136,128]{1,0:T(8,128)S(1)}, f32[136,128]{1,0:T(8,128)S(1)}, u32[]{:S(2)}, u32[]{:S(2)}) collective-permute-start(f32[136,128]{1,0:T(8,128)S(1)} %gather.1.mine_ref), channel_id=1, source_target_pairs={{0,4},{4,0},{1,5},{5,1},{2,6},{6,2},{3,7},{7,3},{8,12},{12,8},{9,1... | collective-permute-start | bytes 208904 | tf_op jit(solution)/shard_map/ppermute | solution.py:313
